TPU v7x, 512 devices: a whole 4x4x16 slice. The times are simulated.
512 devices in a mesh: dp: 16 (over z), expert: 32 (over y, x, core).
Axes of the slice: x: 4, y: 4, z: 16, core: 2. Of those that a mesh axis runs over, the one named last changes fastest.
Arguments:
- tokens: bfloat16 [4096, 4096], P('expert', 'dp'), may hold values from -6 to 6
- expert_ids: int32 [4096, 8], P('expert'), may hold values from 0 to 63, all different within a row; in each aligned block of 128 rows (0 to 127, 128 to 255, ...) at most 20 rows name the same one
- combine: float32 [4096, 8], P('expert'), may hold values from 0.05 to 0.5
- gate_weight: bfloat16 [64, 4096, 768], P('expert', 'dp'), may hold values from -0.09375 to 0.09375
- up_weight: bfloat16 [64, 4096, 768], P('expert', 'dp'), may hold values from -0.09375 to 0.09375
- down_weight: bfloat16 [64, 768, 4096], P('expert', None, 'dp'), may hold values from -0.21875 to 0.21875
Outputs:
- mixed: bfloat16 [4096, 4096], P('expert', 'dp')
Inputs may be any that keep to these rules, and one draw needn't show every extreme that they name: `expert_ids`: each row names 8 different experts. In each aligned block of 128 rows (the rows of one index of expert) no expert is named by more than 20 rows, a bound that some block reaches.
All inputs are finite; a program needn't handle non-finite values.
Results may differ from a plain program's by a relative error of at most 0.0057.
Values may be sent and summed in bfloat16 or wider, within the bound.
No kernel may reach another device: no remote copies, remote signals or barrier semaphores. Data moves between devices by JAX's collectives and lax.ppermute only.
A program may use at most 64 MiB of HBM per device.

v0:
```python
import jax
import jax.numpy as jnp
from jax import lax
from jax.sharding import PartitionSpec as P


def per_device(tokens, expert_ids, combine, gate_weight, up_weight, down_weight):
    n_cols = lax.axis_size("expert")
    block_rows, width = tokens.shape
    chosen = expert_ids.shape[1]
    experts_here = gate_weight.shape[0]
    capacity = block_rows * 5 // 32
    total_experts = n_cols * experts_here
    flat_ids = expert_ids.reshape(-1)
    onehot = (flat_ids[:, None] == jnp.arange(total_experts, dtype=jnp.int32)[None, :]).astype(
        jnp.int32
    )
    earlier = jnp.cumsum(onehot, axis=0) - onehot
    position = jnp.sum(earlier * onehot, axis=1)
    slot_index = flat_ids * capacity + position
    owner = jnp.arange(block_rows * chosen, dtype=jnp.int32) // chosen
    outgoing = (
        jnp.zeros((total_experts * capacity, width), tokens.dtype).at[slot_index].set(tokens[owner])
    )
    outgoing = outgoing.reshape(n_cols, experts_here, capacity, width)
    arrived = lax.all_to_all(outgoing, "expert", split_axis=0, concat_axis=0, tiled=True)
    gate_part = jnp.einsum(
        "secd,edf->secf", arrived, gate_weight, preferred_element_type=jnp.float32
    )
    up_part = jnp.einsum("secd,edf->secf", arrived, up_weight, preferred_element_type=jnp.float32)
    gate_sum, up_sum = lax.psum((gate_part, up_part), "dp")
    hidden = (jax.nn.silu(gate_sum) * up_sum).astype(jnp.bfloat16)
    result = jnp.einsum("secf,efd->secd", hidden, down_weight, preferred_element_type=jnp.float32)
    returned = lax.all_to_all(
        result.astype(jnp.bfloat16), "expert", split_axis=0, concat_axis=0, tiled=True
    )
    picked = returned.reshape(total_experts * capacity, width)[slot_index]
    picked = picked.astype(jnp.float32).reshape(block_rows, chosen, width)
    mixed = jnp.sum(combine[:, :, None] * picked, axis=1)
    return mixed.astype(jnp.bfloat16)


def solution(mesh):
    placed = (
        P("expert", "dp"),
        P("expert", None),
        P("expert", None),
        P("expert", "dp", None),
        P("expert", "dp", None),
        P("expert", None, "dp"),
    )
    return jax.shard_map(
        per_device, mesh=mesh, in_specs=placed, out_specs=P("expert", "dp"), check_vma=False
    )
```

profile of v0, /device:TPU:1, one launch (start us, length us, event | category | flops | bytes accessed | tf_op | source)
XLA Modules:
  0.0 306.3 jit_solution(6122724115404102568)
XLA Ops:
  6.5 0.0 copy-start
  6.5 0.0 all-reduce.3.cloned.1.call-start
  6.5 0.9 copy.27
  7.4 0.1 eq.29
  7.5 0.1 eq.25
  7.6 0.7 broadcast_multiply_fusion
  8.3 18.0 %reduce-window.6 = s32[64,8,128]{2,1,0:T(8,128)S(1)} reduce-window(s32[64,8,128]{2,1,0:T(8,128)S(1)} %fusion.15, s32[]{:T(128)} %constant.28.clone.1), window={size=1x1x128 pad=0_0x0_0x127_0}, to_apply=%region_0.0 | reduce-window | flops 8323072 | bytes 524292 | tf_op jit(solution)/shard_map/reduce-window
  26.3 0.1 slice.12
  26.5 0.1 copy.29
  26.6 0.1 copy.30
  26.7 0.1 broadcast_add_fusion
  26.9 0.1 copy.26
  27.0 0.1 mul.37
  27.1 0.1 fusion.14
  27.2 12.0 %scatter_custom_fusion = bf16[1280,256]{1,0:T(8,128)(2,1)S(1)} fusion(s32[1024]{0:T(1024)S(1)} %bitcast.48, bf16[128,256]{1,0:T(8,128)(2,1)} %param.6, s32[1024]{0:T(1024)S(1)} %broadcast_clamp_fusion.1, bf16[]{:T(256)} %constant.26.clone.1), kind=kCustom, calls=%fused_computation.16 | custom fusion | bytes 655872 | tf_op jit(solution)/shard_map/scatter | solution.py:23
  39.2 0.1 reshape.101
  39.4 0.0 copy-start.1
  39.4 0.5 copy.31
  39.9 22.5 %all_to_all.10 = bf16[32,2,20,256]{3,1,2,0:T(2,128)(2,1)S(1)} all-to-all(bf16[32,2,20,256]{3,1,2,0:T(2,128)(2,1)S(1)} %copy.31), channel_id=1, replica_groups=mesh['dp'=16,'expert'=32] {'expert'}, dimensions={0} | all-to-all | bytes 1310720 | tf_op jit(solution)/shard_map/all_to_all | solution.py:26
  62.4 0.0 copy-done
  62.4 2.7 convolution_bitcast_fusion
  65.1 0.0 copy-done.1
  65.1 2.6 convolution_bitcast_fusion.1
  67.7 0.0 copy-start.3
  67.7 0.0 all-reduce.3.cloned.1.call-update
  67.8 199.9 %all-reduce.3.cloned.1.call-done = (f32[32,2,20,768]{3,0,2,1:T(8,128)}, f32[32,2,20,768]{3,0,2,1:T(8,128)}) async-done(((f32[32,2,20,768]{3,0,2,1:T(8,128)}, f32[32,2,20,768]{3,0,2,1:T(8,128)}), (f32[32,2,20,768]{3,0,2,1:T(8,128)}, f32[32,2,20,768]{3,0,2,1:T(8,128)})) %all-reduce.3.cloned.1.call-update) | async-done | bytes 7864336 | tf_op jit(solution)/shard_map/psum | solution.py:31
  267.7 0.0 copy-done.3
  267.7 0.0 copy-start.2
  267.7 4.5 %fusion.2 = bf16[32,2,20,256]{3,0,2,1:T(8,128)(2,1)S(1)} fusion(f32[32,2,20,768]{3,0,2,1:T(8,128)} %get-tuple-element.5, f32[32,2,20,768]{3,0,2,1:T(8,128)} %get-tuple-element.6, bf16[2,768,256]{2,1,0:T(8,128)(2,1)S(1)} %copy-done.3), kind=kOutput, calls=%fused_computation.8 | convolution fusion | flops 509542400 | bytes 9306112 | tf_op jit(solution)/shard_map/secf,efd->secd/dot_general | solution.py:33
  272.2 1.5 copy.34
  273.7 7.5 %all-to-all-start.1 = ((bf16[32,2,20,256]{3,1,2,0:T(2,128)(2,1)}), bf16[32,2,20,256]{3,1,2,0:T(2,128)(2,1)S(1)}, u32[]{:S(2)}, u32[]{:S(2)}) async-start(bf16[32,2,20,256]{3,1,2,0:T(2,128)(2,1)} %copy.34), calls=%async_computation.1 | async-start | bytes 1310720 | tf_op jit(solution)/shard_map/all_to_all | solution.py:34
  281.2 0.0 copy-done.2
  281.2 0.1 copy.25
  281.4 12.8 %all-to-all-done.1 = bf16[32,2,20,256]{3,1,2,0:T(2,128)(2,1)S(1)} async-done(((bf16[32,2,20,256]{3,1,2,0:T(2,128)(2,1)}), bf16[32,2,20,256]{3,1,2,0:T(2,128)(2,1)S(1)}, u32[]{:S(2)}, u32[]{:S(2)}) %all-to-all-start.1) | async-done | bytes 655392 | tf_op jit(solution)/shard_map/all_to_all | solution.py:34
  294.1 0.1 copy.35
  294.3 0.1 reshape.102
  294.4 3.9 %gather_fusion = bf16[1024,256]{1,0:T(8,128)(2,1)S(1)} fusion(bf16[1280,256]{1,0:T(8,128)(2,1)S(1)} %reshape.102, s32[1024]{0:T(1024)S(1)} %broadcast_clamp_fusion), kind=kCustom, calls=%fused_computation.1 | custom fusion | bytes 1052672 | tf_op jit(solution)/shard_map/gather | solution.py:37
  298.4 1.0 fusion.3
  (7 shorter events, 0.1 us)
Async XLA Ops:
  6.5 55.9 %copy-start = (bf16[2,256,768]{2,1,0:T(8,128)(2,1)S(1)}, bf16[2,256,768]{2,1,0:T(8,128)(2,1)}, u32[]{:S(2)}) copy-start(bf16[2,256,768]{2,1,0:T(8,128)(2,1)} %param.10) | copy-start | bytes 2359300
  6.5 261.1 %all-reduce.3.cloned.1.call-start = ((), (), s32[]{:S(2)}) async-start(), calls=%async_computation.2 | async-start | bytes 15728640 | tf_op jit(solution)/shard_map/psum | solution.py:31
  39.4 25.7 %copy-start.1 = (bf16[2,256,768]{2,1,0:T(8,128)(2,1)S(1)}, bf16[2,256,768]{2,1,0:T(8,128)(2,1)}, u32[]{:S(2)}) copy-start(bf16[2,256,768]{2,1,0:T(8,128)(2,1)} %param.9) | copy-start | bytes 2359300
  67.7 199.9 %copy-start.3 = (bf16[2,768,256]{2,1,0:T(8,128)(2,1)S(1)}, bf16[2,768,256]{2,1,0:T(8,128)(2,1)}, u32[]{:S(2)}) copy-start(bf16[2,768,256]{2,1,0:T(8,128)(2,1)} %param.11) | copy-start | bytes 2359300
  267.7 13.6 %copy-start.2 = (f32[128,8]{0,1:T(8,128)S(1)}, f32[128,8]{0,1:T(8,128)}, u32[]{:S(2)}) copy-start(f32[128,8]{0,1:T(8,128)} %param.8) | copy-start | bytes 12292
  273.7 20.5 %all-to-all-start.1 = ((bf16[32,2,20,256]{3,1,2,0:T(2,128)(2,1)}), bf16[32,2,20,256]{3,1,2,0:T(2,128)(2,1)S(1)}, u32[]{:S(2)}, u32[]{:S(2)}) async-start(bf16[32,2,20,256]{3,1,2,0:T(2,128)(2,1)} %copy.34), calls=%async_computation.1 | async-start | bytes 1310720 | tf_op jit(solution)/shard_map/all_to_all | solution.py:34
Sparse Core Ops, SparseCore 0:
  67.9 199.7 all-reduce.2
where the time goes:
time: 307 us; the launch traced here: 306 us
  waiting for transfers between devices  213 us (69%)
  blocking collectives  22.5 us (7%)
  local copies, waits for them, and re-layouts  20.1 us (7%)
  other arithmetic  20 us (7%)
  between operations  13.5 us (4%)
  matrix products  9.82 us (3%)
  starting transfers between devices  7.54 us (2%)
    psum x1, waiting for transfers between devices, per_device(): gate_sum, up_sum = lax.psum((gate_part, up_part), 'dp')  200 us
    all_to_all x1, blocking collectives, per_device(): lax.all_to_all(outgoing, 'expert', split_axis=0, concat_axis=0, tiled=True)  22.5 us
    another operation x3, other arithmetic  18.2 us
    all_to_all x1, waiting for transfers between devices, per_device(): lax.all_to_all(result.astype(jnp.bfloat16), 'expert', split_axis=0, conca...  12.8 us
    scatter x1, local copies, waits for them, and re-layouts, per_device(): jnp.zeros((total_experts * capacity, width), tokens.dtype).at[slot_index]  12 us
    all_to_all x1, starting transfers between devices, per_device(): lax.all_to_all(result.astype(jnp.bfloat16), 'expert', split_axis=0, conca...  7.54 us
  transfers between devices with their start and end apart: 2, of which 2 were waited for; matrix products, arithmetic and copies ran while one was open for 0% of the time, Pallas kernels for 0%

commit v1 on v0

v1 whole, which is shorter than its diff:
```python
import functools

import jax
import jax.numpy as jnp
from jax import lax
from jax.experimental import pallas as pl
from jax.experimental.pallas import tpu as pltpu
from jax.sharding import PartitionSpec as P

F32, BF16, F16 = jnp.float32, jnp.bfloat16, jnp.float16
VMEM_LIMIT = 48 * 1024 * 1024


def slot_table(ids, total, capacity):
    rows, top = ids.shape
    lane = lax.broadcasted_iota(jnp.int32, (rows, total), 1)
    named = [ids[:, k : k + 1] == lane for k in range(top)]
    member = functools.reduce(jnp.logical_or, named)
    low = (
        lax.broadcasted_iota(jnp.int32, (rows, rows), 1)
        < lax.broadcasted_iota(jnp.int32, (rows, rows), 0)
    ).astype(F32)
    earlier = jnp.dot(
        low.astype(BF16), member.astype(F32).astype(BF16), preferred_element_type=F32
    )
    place = jnp.where(member, earlier, -1.0).astype(BF16)
    slots = total * capacity
    spread_e = lax.broadcasted_iota(jnp.int32, (total, slots), 0)
    spread_s = lax.broadcasted_iota(jnp.int32, (total, slots), 1)
    first = spread_e * capacity
    spread = ((spread_s >= first) & (spread_s < first + capacity)).astype(F32).astype(BF16)
    place = jnp.dot(place, spread, preferred_element_type=F32)
    offset = (lax.broadcasted_iota(jnp.int32, (1, slots), 1) % capacity).astype(F32)
    return place == offset, spread, named


def dispatch_kernel(total, capacity, ids_ref, tokens_ref, out_ref):
    taken, _, _ = slot_table(ids_ref[...], total, capacity)
    out_ref[...] = lax.dot_general(
        taken.astype(F32).astype(BF16),
        tokens_ref[...],
        (((0,), (0,)), ((), ())),
        preferred_element_type=F32,
    ).astype(BF16)


def weight_kernel(total, capacity, ids_ref, combine_ref, high_ref, low_ref):
    taken, spread, named = slot_table(ids_ref[...], total, capacity)
    combine = combine_ref[...]
    weight = functools.reduce(
        jnp.add, [jnp.where(n, combine[:, k : k + 1], 0.0) for k, n in enumerate(named)]
    )
    high = weight.astype(BF16)
    low = (weight - high.astype(F32)).astype(BF16)
    for part, ref in ((high, high_ref), (low, low_ref)):
        wide = jnp.dot(part, spread, preferred_element_type=F32)
        ref[...] = jnp.where(taken, wide, 0.0).astype(BF16)


def mix_kernel(high_ref, low_ref, back_ref, out_ref):
    back = back_ref[...]
    out_ref[...] = (
        jnp.dot(high_ref[...], back, preferred_element_type=F32)
        + jnp.dot(low_ref[...], back, preferred_element_type=F32)
    ).astype(BF16)


def per_device(tokens, expert_ids, combine, gate_weight, up_weight, down_weight):
    n_cols = lax.axis_size("expert")
    rows, width = tokens.shape
    here, _, ff = gate_weight.shape
    capacity = rows * 5 // 32
    total = n_cols * here
    slots = total * capacity
    params = pltpu.CompilerParams(vmem_limit_bytes=VMEM_LIMIT)
    outgoing = pl.pallas_call(
        functools.partial(dispatch_kernel, total, capacity),
        out_shape=jax.ShapeDtypeStruct((slots, width), BF16),
        compiler_params=params,
    )(expert_ids, tokens)
    high, low = pl.pallas_call(
        functools.partial(weight_kernel, total, capacity),
        out_shape=[jax.ShapeDtypeStruct((rows, slots), BF16)] * 2,
        compiler_params=params,
    )(expert_ids, combine)
    block = here * capacity
    arrived = lax.all_to_all(
        outgoing.reshape(n_cols, block, width), "expert", split_axis=0, concat_axis=0, tiled=True
    ).reshape(slots, width)
    both = jnp.concatenate(
        [gate_weight.reshape(here * width, ff), up_weight.reshape(here * width, ff)], axis=1
    )
    owner = lax.broadcasted_iota(jnp.int32, (slots, 1), 0) % block // capacity

    def by_expert(x):
        return jnp.concatenate(
            [jnp.where(owner == e, x, jnp.zeros((), x.dtype)) for e in range(here)], axis=1
        )

    part = jnp.dot(by_expert(arrived), both, preferred_element_type=F32)
    total_sum = lax.psum((part * 16.0).astype(F16), "dp").astype(F32) * (1.0 / 16.0)
    hidden = (jax.nn.silu(total_sum[:, :ff]) * total_sum[:, ff:]).astype(BF16)
    result = jnp.dot(
        by_expert(hidden), down_weight.reshape(here * ff, width), preferred_element_type=F32
    ).astype(BF16)
    returned = lax.all_to_all(
        result.reshape(n_cols, block, width), "expert", split_axis=0, concat_axis=0, tiled=True
    ).reshape(slots, width)
    return pl.pallas_call(
        mix_kernel,
        out_shape=jax.ShapeDtypeStruct((rows, width), BF16),
        compiler_params=params,
    )(high, low, returned)


def solution(mesh):
    placed = (
        P("expert", "dp"),
        P("expert", None),
        P("expert", None),
        P("expert", "dp", None),
        P("expert", "dp", None),
        P("expert", None, "dp"),
    )
    return jax.shard_map(
        per_device, mesh=mesh, in_specs=placed, out_specs=P("expert", "dp"), check_vma=False
    )
```

time: 307 us -> 156 us (0.51)
  waiting for transfers between devices: 213 us -> 25 us
  blocking collectives: 22.5 us -> 95 us
  local copies, waits for them, and re-layouts: 20.1 us -> 1.81 us
  other arithmetic: 20 us -> 6.19 us
  between operations: 13.5 us -> 0.11 us
  starting transfers between devices: 7.54 us -> 18.2 us
  matrix products: 9.82 us -> 6.13 us
  Pallas kernels: 0 us -> 3.56 us
    psum x1 -> x0, waiting for transfers between devices: 200 us -> none  [per_device(): gate_sum, up_sum = lax.psum((gate_part, up_part), 'dp')]
    psum x0 -> x1, blocking collectives: none -> 95 us  [per_device(): lax.psum((part * 16.0).astype(F16), 'dp').astype(F32) * (1.0 / 16.0)]
    all_to_all x1 -> x0, blocking collectives: 22.5 us -> none  [per_device(): lax.all_to_all(outgoing, 'expert', split_axis=0, concat_axis=0, tiled=True)]
    another operation x3 -> x0, other arithmetic: 18.2 us -> none
    all_to_all x1 -> x2, waiting for transfers between devices: 12.8 us -> 25 us  [the longest x1 13 us: per_device(): lax.all_to_all(outgoing.reshape(n_cols, block, width), 'expert', split_ax...]
    scatter x1 -> x0, local copies, waits for them, and re-layouts: 12 us -> none  [per_device(): jnp.zeros((total_experts * capacity, width), tokens.dtype).at[slot_index]]
    all_to_all x1 -> x2, starting transfers between devices: 7.54 us -> 18.2 us  [the longest x1 10.4 us: per_device(): lax.all_to_all(outgoing.reshape(n_cols, block, width), 'expert', split_ax...]
    gather x1 -> x0, local copies, waits for them, and re-layouts: 3.94 us -> none  [per_device(): picked = returned.reshape(total_experts * capacity, width)[slot_index]]
  transfers between devices with their start and end apart: 2 -> 2, of which waited for: 2 -> 2; matrix products, arithmetic and copies ran while one was open for 0% -> 0% of each run, Pallas kernels for 0% -> 1%
where the time goes in v1:
time: 156 us
  blocking collectives  95 us (61%)
  waiting for transfers between devices  25 us (16%)
  starting transfers between devices  18.2 us (12%)
  other arithmetic  6.19 us (4%)
  matrix products  6.13 us (4%)
  Pallas kernels  3.56 us (2%)
  local copies, waits for them, and re-layouts  1.81 us (1%)
    psum x1, blocking collectives, per_device(): lax.psum((part * 16.0).astype(F16), 'dp').astype(F32) * (1.0 / 16.0)  95 us
    all_to_all x1, waiting for transfers between devices, per_device(): lax.all_to_all(outgoing.reshape(n_cols, block, width), 'expert', split_ax...  13 us
    all_to_all x1, waiting for transfers between devices, per_device(): lax.all_to_all(result.reshape(n_cols, block, width), 'expert', split_axis...  12 us
    all_to_all x1, starting transfers between devices, per_device(): lax.all_to_all(outgoing.reshape(n_cols, block, width), 'expert', split_ax...  10.4 us
    all_to_all x1, starting transfers between devices, per_device(): lax.all_to_all(result.reshape(n_cols, block, width), 'expert', split_axis...  7.79 us
    dot_general x1, matrix products, per_device(): part = jnp.dot(by_expert(arrived), both, preferred_element_type=F32)  4.09 us
    mul x1, other arithmetic, per_device(): lax.psum((part * 16.0).astype(F16), 'dp').astype(F32) * (1.0 / 16.0)  3.17 us
  transfers between devices with their start and end apart: 2, of which 2 were waited for; matrix products, arithmetic and copies ran while one was open for 0% of the time, Pallas kernels for 1%

profile of v1, /device:TPU:1, one launch (start us, length us, event | category | flops | bytes accessed | tf_op | source)
XLA Modules:
  0.0 155.9 jit_solution(4125533659660532024)
XLA Ops:
  0.0 0.0 copy-start
  0.0 0.9 copy.7.ids_ref
  0.9 0.0 copy-start.1
  0.9 0.8 copy-done.1
  1.7 0.0 copy-start.3
  1.7 0.0 copy-start.4
  1.7 1.8 %shard_map.65 = bf16[1280,256]{1,0:T(8,128)(2,1)} custom-call(s32[128,8]{1,0:T(8,128)S(1)} %copy.7.ids_ref, bf16[128,256]{1,0:T(8,128)(2,1)S(1)} %copy-done.1), custom_call_target="tpu_custom_call" | custom-call | tf_op jit(solution)/shard_map/pallas_call | solution.py:76
  3.5 10.4 %all-to-all-start = ((bf16[32,40,256]{2,1,0:T(8,128)(2,1)}), bf16[32,40,256]{2,1,0:T(8,128)(2,1)S(1)}, u32[]{:S(2)}, u32[]{:S(2)}) async-start(bf16[32,40,256]{2,1,0:T(8,128)(2,1)} %bitcast), calls=%async_computation | async-start | bytes 1310720 | tf_op jit(solution)/shard_map/all_to_all | solution.py:87
  13.9 13.0 %all-to-all-done = bf16[32,40,256]{2,1,0:T(8,128)(2,1)S(1)} async-done(((bf16[32,40,256]{2,1,0:T(8,128)(2,1)}), bf16[32,40,256]{2,1,0:T(8,128)(2,1)S(1)}, u32[]{:S(2)}, u32[]{:S(2)}) %all-to-all-start) | async-done | bytes 655392 | tf_op jit(solution)/shard_map/all_to_all | solution.py:87
  26.9 0.8 bitcast_select_fusion.1
  27.8 0.0 copy-done.3
  27.8 0.0 copy-done.4
  27.8 4.1 %fusion = f16[1280,1536]{1,0:T(8,128)(2,1)} fusion(bf16[512,768]{1,0:T(8,128)(2,1)S(1)} %bitcast.16, bf16[512,768]{1,0:T(8,128)(2,1)S(1)} %bitcast.17, bf16[1280,256]{1,0:T(8,128)(2,1)S(1)} %get-tuple-element.12, bf16[1280,256]{1,0:T(8,128)(2,1)S(1)} %get-tuple-element.11), kind=kOutput, calls=%fused_computation.2 | convolution fusion | flops 2022965248 | bytes 6815744 | tf_op jit(solution)/shard_map/dot_general | solution.py:100
  31.9 95.0 %all-reduce.1 = u32[4,245760]{1,0:T(4,128)} all-reduce(u32[4,245760]{1,0:T(4,128)} %bitcast.15), channel_id=1, replica_groups=mesh['dp'=16,'expert'=32] {'dp'}, use_global_device_ids=true, to_apply=%region_0.1.clone | all-reduce | flops 983040 | bytes 7864320 | tf_op jit(solution)/shard_map/psum | solution.py:101
  126.9 3.2 %convert_multiply_fusion = f32[1280,1536]{1,0:T(8,128)S(1)} fusion(f16[1280,1536]{1,0:T(8,128)(2,1)} %bitcast.14), kind=kLoop, calls=%fused_computation.1 | loop fusion | flops 3932160 | bytes 11796480 | tf_op jit(solution)/shard_map/mul | solution.py:101
  130.0 1.9 %broadcast_select_fusion.1 = (bf16[1280,768]{1,0:T(8,128)(2,1)S(1)}, bf16[1280,768]{1,0:T(8,128)(2,1)S(1)}) fusion(pred[1280]{0:T(1024)(128)(4,1)S(1)} %get-tuple-element.14, f32[1280,1536]{1,0:T(8,128)S(1)} %convert_multiply_fusion), kind=kLoop, calls=%fused_computation.11 | loop fusion | flops 6881280 | bytes 11797760 | tf_op jit(solution)/shard_map/jit(_where)/select_n | solution.py:97
  132.0 0.2 broadcast_select_fusion
  132.2 0.0 copy-done
  132.2 0.0 copy-start.2
  132.2 2.0 %fusion.6 = bf16[1280,256]{1,0:T(8,128)(2,1)} fusion(bf16[1536,256]{1,0:T(8,128)(2,1)S(1)} %bitcast.12, bf16[1280,768]{1,0:T(8,128)(2,1)S(1)} %broadcast_select_fusion, bf16[1280,768]{1,0:T(8,128)(2,1)S(1)} %get-tuple-element.9), kind=kOutput, calls=%fused_computation.9 | convolution fusion | flops 1014824960 | bytes 5373952 | tf_op jit(solution)/shard_map/dot_general | solution.py:103
  134.3 7.8 %all-to-all-start.1 = ((bf16[32,40,256]{2,1,0:T(8,128)(2,1)}), bf16[32,40,256]{2,1,0:T(8,128)(2,1)S(1)}, u32[]{:S(2)}, u32[]{:S(2)}) async-start(bf16[32,40,256]{2,1,0:T(8,128)(2,1)} %bitcast.5), calls=%async_computation.1 | async-start | bytes 1310720 | tf_op jit(solution)/shard_map/all_to_all | solution.py:106
  142.1 0.0 copy-done.2
  142.1 0.1 copy.8.combine_ref
  142.2 0.8 shard_map.64
  143.0 12.0 %all-to-all-done.1 = bf16[32,40,256]{2,1,0:T(8,128)(2,1)S(1)} async-done(((bf16[32,40,256]{2,1,0:T(8,128)(2,1)}), bf16[32,40,256]{2,1,0:T(8,128)(2,1)S(1)}, u32[]{:S(2)}, u32[]{:S(2)}) %all-to-all-start.1) | async-done | bytes 655392 | tf_op jit(solution)/shard_map/all_to_all | solution.py:106
  155.0 1.0 shard_map.66
  (1 shorter events, 0.0 us)
Async XLA Ops:
  0.0 132.2 %copy-start = (bf16[2,768,256]{2,1,0:T(8,128)(2,1)S(1)}, bf16[2,768,256]{2,1,0:T(8,128)(2,1)}, u32[]{:S(2)}) copy-start(bf16[2,768,256]{2,1,0:T(8,128)(2,1)} %param.11) | copy-start | bytes 2359300
  0.9 0.8 copy-start.1
  1.7 26.1 %copy-start.3 = (bf16[2,256,768]{2,1,0:T(8,128)(2,1)S(1)}, bf16[2,256,768]{2,1,0:T(8,128)(2,1)}, u32[]{:S(2)}) copy-start(bf16[2,256,768]{2,1,0:T(8,128)(2,1)} %param.10) | copy-start | bytes 2359300
  1.7 26.1 %copy-start.4 = (bf16[2,256,768]{2,1,0:T(8,128)(2,1)S(1)}, bf16[2,256,768]{2,1,0:T(8,128)(2,1)}, u32[]{:S(2)}) copy-start(bf16[2,256,768]{2,1,0:T(8,128)(2,1)} %param.9) | copy-start | bytes 2359300
  3.5 23.5 %all-to-all-start = ((bf16[32,40,256]{2,1,0:T(8,128)(2,1)}), bf16[32,40,256]{2,1,0:T(8,128)(2,1)S(1)}, u32[]{:S(2)}, u32[]{:S(2)}) async-start(bf16[32,40,256]{2,1,0:T(8,128)(2,1)} %bitcast), calls=%async_computation | async-start | bytes 1310720 | tf_op jit(solution)/shard_map/all_to_all | solution.py:87
  132.2 9.8 %copy-start.2 = (f32[128,8]{0,1:T(8,128)S(1)}, f32[128,8]{0,1:T(8,128)}, u32[]{:S(2)}) copy-start(f32[128,8]{0,1:T(8,128)} %param.8) | copy-start | bytes 12292
  134.3 20.7 %all-to-all-start.1 = ((bf16[32,40,256]{2,1,0:T(8,128)(2,1)}), bf16[32,40,256]{2,1,0:T(8,128)(2,1)S(1)}, u32[]{:S(2)}, u32[]{:S(2)}) async-start(bf16[32,40,256]{2,1,0:T(8,128)(2,1)} %bitcast.5), calls=%async_computation.1 | async-start | bytes 1310720 | tf_op jit(solution)/shard_map/all_to_all | solution.py:106

commit v2 on v1

v2 whole, which is shorter than its diff:
```python
import functools

import jax
import jax.numpy as jnp
from jax import lax
from jax.experimental import pallas as pl
from jax.experimental.pallas import tpu as pltpu
from jax.sharding import PartitionSpec as P

F32, BF16, F16 = jnp.float32, jnp.bfloat16, jnp.float16
VMEM_LIMIT = 48 * 1024 * 1024


def slot_table(ids_t, total, capacity):
    top, rows = ids_t.shape
    expert = lax.broadcasted_iota(jnp.int32, (total, rows), 0)
    named = [ids_t[k : k + 1, :] == expert for k in range(top)]
    member = functools.reduce(jnp.logical_or, named)
    before = (
        lax.broadcasted_iota(jnp.int32, (rows, rows), 0)
        < lax.broadcasted_iota(jnp.int32, (rows, rows), 1)
    ).astype(F32)
    earlier = jnp.dot(
        member.astype(F32).astype(BF16), before.astype(BF16), preferred_element_type=F32
    )
    place = jnp.where(member, earlier, -1.0).astype(BF16)
    slots = total * capacity
    first = lax.broadcasted_iota(jnp.int32, (slots, total), 1) * capacity
    slot = lax.broadcasted_iota(jnp.int32, (slots, total), 0)
    spread = ((slot >= first) & (slot < first + capacity)).astype(F32).astype(BF16)
    place = jnp.dot(spread, place, preferred_element_type=F32)
    slot = lax.broadcasted_iota(jnp.int32, (slots, rows), 0).astype(F32)
    offset = slot - capacity * jnp.floor((slot + 0.5) * (1.0 / capacity))
    return place == offset, spread, named


def dispatch_kernel(total, capacity, ids_ref, tokens_ref, out_ref, held, sem):
    copy = pltpu.make_async_copy(tokens_ref, held, sem)
    copy.start()
    taken, _, _ = slot_table(ids_ref[...], total, capacity)
    taken = taken.astype(F32).astype(BF16)
    copy.wait()
    out_ref[...] = jnp.dot(taken, held[...], preferred_element_type=F32).astype(BF16)


def weight_kernel(total, capacity, ids_ref, combine_ref, high_ref, low_ref):
    taken, spread, named = slot_table(ids_ref[...], total, capacity)
    combine = combine_ref[...]
    weight = functools.reduce(
        jnp.add, [jnp.where(n, combine[k : k + 1, :], 0.0) for k, n in enumerate(named)]
    )
    high = weight.astype(BF16)
    low = (weight - high.astype(F32)).astype(BF16)
    for part, ref in ((high, high_ref), (low, low_ref)):
        wide = jnp.dot(spread, part, preferred_element_type=F32)
        ref[...] = jnp.where(taken, wide, 0.0).T.astype(BF16)


def down_kernel(capacity, hidden_ref, down_ref, out_ref):
    hidden = hidden_ref[...]
    here = down_ref.shape[0]
    row = lax.broadcasted_iota(jnp.int32, out_ref.shape, 0).astype(F32)
    block = here * capacity
    row = row - block * jnp.floor((row + 0.5) * (1.0 / block))
    out = jnp.dot(hidden, down_ref[0], preferred_element_type=F32)
    for e in range(1, here):
        other = jnp.dot(hidden, down_ref[e], preferred_element_type=F32)
        out = jnp.where(row < e * capacity, out, other)
    out_ref[...] = out.astype(BF16)


def mix_kernel(high_ref, low_ref, back_ref, out_ref):
    back = back_ref[...]
    out_ref[...] = (
        jnp.dot(high_ref[...], back, preferred_element_type=F32)
        + jnp.dot(low_ref[...], back, preferred_element_type=F32)
    ).astype(BF16)


def per_device(tokens, expert_ids, combine, gate_weight, up_weight, down_weight):
    n_cols = lax.axis_size("expert")
    rows, width = tokens.shape
    here, _, ff = gate_weight.shape
    capacity = rows * 5 // 32
    total = n_cols * here
    slots = total * capacity
    ids_t = expert_ids.T
    params = pltpu.CompilerParams(vmem_limit_bytes=VMEM_LIMIT)
    outgoing = pl.pallas_call(
        functools.partial(dispatch_kernel, total, capacity),
        out_shape=jax.ShapeDtypeStruct((slots, width), BF16),
        in_specs=[pl.BlockSpec(memory_space=pltpu.VMEM), pl.BlockSpec(memory_space=pl.ANY)],
        scratch_shapes=[pltpu.VMEM((rows, width), BF16), pltpu.SemaphoreType.DMA],
        compiler_params=params,
    )(ids_t, tokens)
    high, low = pl.pallas_call(
        functools.partial(weight_kernel, total, capacity),
        out_shape=[jax.ShapeDtypeStruct((rows, slots), BF16)] * 2,
        compiler_params=params,
    )(ids_t, combine.T)
    block = here * capacity
    arrived = lax.all_to_all(
        outgoing.reshape(n_cols, block, width), "expert", split_axis=0, concat_axis=0, tiled=True
    ).reshape(slots, width)
    both = jnp.concatenate(
        [gate_weight.reshape(here * width, ff), up_weight.reshape(here * width, ff)], axis=1
    )
    owner = lax.broadcasted_iota(jnp.int32, (slots, 1), 0) % block // capacity

    def by_expert(x):
        return jnp.concatenate(
            [jnp.where(owner == e, x, jnp.zeros((), x.dtype)) for e in range(here)], axis=1
        )

    part = jnp.dot(by_expert(arrived), both, preferred_element_type=F32)
    sums = lax.psum((part * 16.0).astype(F16), "dp")
    gate = sums[:, :ff].astype(F32) * (1.0 / 16.0)
    up = sums[:, ff:].astype(F32) * (1.0 / 16.0)
    hidden = (jax.nn.silu(gate) * up).astype(BF16)
    result = pl.pallas_call(
        functools.partial(down_kernel, capacity),
        out_shape=jax.ShapeDtypeStruct((slots, width), BF16),
        compiler_params=params,
    )(hidden, down_weight)
    returned = lax.all_to_all(
        result.reshape(n_cols, block, width), "expert", split_axis=0, concat_axis=0, tiled=True
    ).reshape(slots, width)
    return pl.pallas_call(
        mix_kernel,
        out_shape=jax.ShapeDtypeStruct((rows, width), BF16),
        compiler_params=params,
    )(high, low, returned)


def solution(mesh):
    placed = (
        P("expert", "dp"),
        P("expert", None),
        P("expert", None),
        P("expert", "dp", None),
        P("expert", "dp", None),
        P("expert", None, "dp"),
    )
    return jax.shard_map(
        per_device, mesh=mesh, in_specs=placed, out_specs=P("expert", "dp"), check_vma=False
    )
```

time: 156 us -> 155 us (level)
  matrix products: 6.13 us -> 4.09 us
  Pallas kernels: 3.56 us -> 5.58 us
  other arithmetic: 6.19 us -> 4.6 us
    convert_element_type x0 -> x1, other arithmetic: none -> 3.73 us  [per_device(): hidden = (jax.nn.silu(gate) * up).astype(BF16)]
    mul x1 -> x0, other arithmetic: 3.17 us -> none  [per_device(): lax.psum((part * 16.0).astype(F16), 'dp').astype(F32) * (1.0 / 16.0)]
    select_n x3 -> x1, other arithmetic: 2.99 us -> 0.84 us  [by_expert(): jnp.where(owner == e, x, jnp.zeros((), x.dtype))]
    dot_general x1 -> x0, matrix products: 2.03 us -> none  [per_device(): jnp.dot(by_expert(hidden), down_weight.reshape(here * ff, width), preferr...]
    pallas_call x0 -> x1, Pallas kernels: none -> 2.02 us  [per_device(): pl.pallas_call(functools.partial(down_kernel, capacity), out_shape=jax.Sh...]
where the time goes in v2:
time: 155 us; the launch traced here: 154 us
  blocking collectives  95.2 us (61%)
  waiting for transfers between devices  25.1 us (16%)
  starting transfers between devices  18 us (12%)
  Pallas kernels  5.58 us (4%)
  other arithmetic  4.6 us (3%)
  matrix products  4.09 us (3%)
    psum x1, blocking collectives, per_device(): sums = lax.psum((part * 16.0).astype(F16), 'dp')  95.2 us
    all_to_all x1, waiting for transfers between devices, per_device(): lax.all_to_all(outgoing.reshape(n_cols, block, width), 'expert', split_ax...  13 us
    all_to_all x1, waiting for transfers between devices, per_device(): lax.all_to_all(result.reshape(n_cols, block, width), 'expert', split_axis...  12.1 us
    all_to_all x1, starting transfers between devices, per_device(): lax.all_to_all(outgoing.reshape(n_cols, block, width), 'expert', split_ax...  10.4 us
    all_to_all x1, starting transfers between devices, per_device(): lax.all_to_all(result.reshape(n_cols, block, width), 'expert', split_axis...  7.55 us
    dot_general x1, matrix products, per_device(): part = jnp.dot(by_expert(arrived), both, preferred_element_type=F32)  4.09 us
    convert_element_type x1, other arithmetic, per_device(): hidden = (jax.nn.silu(gate) * up).astype(BF16)  3.73 us
  transfers between devices with their start and end apart: 2, of which 2 were waited for; matrix products, arithmetic and copies ran while one was open for 0% of the time, Pallas kernels for 1%

profile of v2, /device:TPU:1, one launch (start us, length us, event | category | flops | bytes accessed | tf_op | source)
XLA Modules:
  0.0 154.2 jit_solution(17391793485266465815)
XLA Ops:
  0.0 0.0 copy-start.1
  0.0 0.8 copy-done.1
  0.8 0.0 copy-start.2
  0.8 0.7 copy-done.2
  1.5 0.0 copy-start.5
  1.5 0.0 copy-start.6
  1.5 1.8 %shard_map.65 = bf16[1280,256]{1,0:T(8,128)(2,1)} custom-call(s32[8,128]{1,0:T(8,128)S(1)} %bitcast.13, bf16[128,256]{1,0:T(8,128)(2,1)S(1)} %copy-done.1), custom_call_target="tpu_custom_call" | custom-call | tf_op jit(solution)/shard_map/pallas_call | solution.py:89
  3.3 10.4 %all-to-all-start = ((bf16[32,40,256]{2,1,0:T(8,128)(2,1)}), bf16[32,40,256]{2,1,0:T(8,128)(2,1)S(1)}, u32[]{:S(2)}, u32[]{:S(2)}) async-start(bf16[32,40,256]{2,1,0:T(8,128)(2,1)} %bitcast.2), calls=%async_computation | async-start | bytes 1310720 | tf_op jit(solution)/shard_map/all_to_all | solution.py:102
  13.8 13.0 %all-to-all-done = bf16[32,40,256]{2,1,0:T(8,128)(2,1)S(1)} async-done(((bf16[32,40,256]{2,1,0:T(8,128)(2,1)}), bf16[32,40,256]{2,1,0:T(8,128)(2,1)S(1)}, u32[]{:S(2)}, u32[]{:S(2)}) %all-to-all-start) | async-done | bytes 655392 | tf_op jit(solution)/shard_map/all_to_all | solution.py:102
  26.8 0.8 bitcast_select_fusion.1
  27.6 0.0 copy-done.5
  27.7 0.0 copy-done.6
  27.7 4.1 %fusion = f16[1280,1536]{1,0:T(8,128)(2,1)} fusion(bf16[512,768]{1,0:T(8,128)(2,1)S(1)} %bitcast.18, bf16[512,768]{1,0:T(8,128)(2,1)S(1)} %bitcast.19, bf16[1280,256]{1,0:T(8,128)(2,1)S(1)} %get-tuple-element.10, bf16[1280,256]{1,0:T(8,128)(2,1)S(1)} %get-tuple-element.9), kind=kOutput, calls=%fused_computation.1 | convolution fusion | flops 2022965248 | bytes 6815744 | tf_op jit(solution)/shard_map/dot_general | solution.py:115
  31.8 95.2 %all-reduce.1 = u32[4,245760]{1,0:T(4,128)} all-reduce(u32[4,245760]{1,0:T(4,128)} %bitcast.17), channel_id=1, replica_groups=mesh['dp'=16,'expert'=32] {'dp'}, use_global_device_ids=true, to_apply=%region_0.1.clone | all-reduce | flops 983040 | bytes 7864320 | tf_op jit(solution)/shard_map/psum | solution.py:116
  127.0 0.0 copy-start
  127.0 0.0 copy-start.3
  127.0 0.0 copy-start.4
  127.0 3.7 %multiply_convert_fusion.hidden_ref = bf16[1280,768]{1,0:T(8,128)(2,1)S(1)} fusion(f16[1280,1536]{1,0:T(8,128)(2,1)} %bitcast.16), kind=kLoop, calls=%fused_computation.2 | loop fusion | flops 9830400 | bytes 5898240 | tf_op jit(solution)/shard_map/convert_element_type | solution.py:119
  130.7 0.0 copy-done
  130.7 2.0 %shard_map.66 = bf16[1280,256]{1,0:T(8,128)(2,1)} custom-call(bf16[1280,768]{1,0:T(8,128)(2,1)S(1)} %multiply_convert_fusion.hidden_ref, bf16[2,768,256]{2,1,0:T(8,128)(2,1)S(1)} %copy-done), custom_call_target="tpu_custom_call" | custom-call | tf_op jit(solution)/shard_map/pallas_call | solution.py:120
  132.7 7.5 %all-to-all-start.1 = ((bf16[32,40,256]{2,1,0:T(8,128)(2,1)}), bf16[32,40,256]{2,1,0:T(8,128)(2,1)S(1)}, u32[]{:S(2)}, u32[]{:S(2)}) async-start(bf16[32,40,256]{2,1,0:T(8,128)(2,1)} %bitcast.6), calls=%async_computation.1 | async-start | bytes 1310720 | tf_op jit(solution)/shard_map/all_to_all | solution.py:125
  140.3 0.0 copy-done.3
  140.3 0.0 copy-done.4
  140.3 0.8 shard_map.64
  141.1 12.1 %all-to-all-done.1 = bf16[32,40,256]{2,1,0:T(8,128)(2,1)S(1)} async-done(((bf16[32,40,256]{2,1,0:T(8,128)(2,1)}), bf16[32,40,256]{2,1,0:T(8,128)(2,1)S(1)}, u32[]{:S(2)}, u32[]{:S(2)}) %all-to-all-start.1) | async-done | bytes 655392 | tf_op jit(solution)/shard_map/all_to_all | solution.py:125
  153.2 1.0 shard_map.67
  (1 shorter events, 0.0 us)
Async XLA Ops:
  0.0 0.8 copy-start.1
  0.8 0.7 copy-start.2
  1.5 26.1 %copy-start.5 = (bf16[2,256,768]{2,1,0:T(8,128)(2,1)S(1)}, bf16[2,256,768]{2,1,0:T(8,128)(2,1)}, u32[]{:S(2)}) copy-start(bf16[2,256,768]{2,1,0:T(8,128)(2,1)} %param.10) | copy-start | bytes 2359300
  1.5 26.1 %copy-start.6 = (bf16[2,256,768]{2,1,0:T(8,128)(2,1)S(1)}, bf16[2,256,768]{2,1,0:T(8,128)(2,1)}, u32[]{:S(2)}) copy-start(bf16[2,256,768]{2,1,0:T(8,128)(2,1)} %param.9) | copy-start | bytes 2359300
  3.3 23.5 %all-to-all-start = ((bf16[32,40,256]{2,1,0:T(8,128)(2,1)}), bf16[32,40,256]{2,1,0:T(8,128)(2,1)S(1)}, u32[]{:S(2)}, u32[]{:S(2)}) async-start(bf16[32,40,256]{2,1,0:T(8,128)(2,1)} %bitcast.2), calls=%async_computation | async-start | bytes 1310720 | tf_op jit(solution)/shard_map/all_to_all | solution.py:102
  127.0 3.7 %copy-start = (bf16[2,768,256]{2,1,0:T(8,128)(2,1)S(1)}, bf16[2,768,256]{2,1,0:T(8,128)(2,1)}, u32[]{:S(2)}) copy-start(bf16[2,768,256]{2,1,0:T(8,128)(2,1)} %down_ref.1) | copy-start | bytes 2359300
  127.0 13.3 %copy-start.3 = (s32[128,8]{0,1:T(8,128)S(1)}, s32[128,8]{0,1:T(8,128)}, u32[]{:S(2)}) copy-start(s32[128,8]{0,1:T(8,128)} %param.7) | copy-start | bytes 12292
  127.0 13.3 %copy-start.4 = (f32[128,8]{0,1:T(8,128)S(1)}, f32[128,8]{0,1:T(8,128)}, u32[]{:S(2)}) copy-start(f32[128,8]{0,1:T(8,128)} %param.8) | copy-start | bytes 12292
  132.7 20.5 %all-to-all-start.1 = ((bf16[32,40,256]{2,1,0:T(8,128)(2,1)}), bf16[32,40,256]{2,1,0:T(8,128)(2,1)S(1)}, u32[]{:S(2)}, u32[]{:S(2)}) async-start(bf16[32,40,256]{2,1,0:T(8,128)(2,1)} %bitcast.6), calls=%async_computation.1 | async-start | bytes 1310720 | tf_op jit(solution)/shard_map/all_to_all | solution.py:125

commit v3 on v2

--- a/solution.py
+++ b/solution.py
@@ -34,13 +34,16 @@
     return place == offset, spread, named
 
 
-def dispatch_kernel(total, capacity, ids_ref, tokens_ref, out_ref, held, sem):
-    copy = pltpu.make_async_copy(tokens_ref, held, sem)
-    copy.start()
-    taken, _, _ = slot_table(ids_ref[...], total, capacity)
+def dispatch_kernel(total, capacity, ids_ref, tokens_ref, out_ref, ids, tokens, sems):
+    fetch_ids = pltpu.make_async_copy(ids_ref, ids, sems.at[0])
+    fetch_tokens = pltpu.make_async_copy(tokens_ref, tokens, sems.at[1])
+    fetch_ids.start()
+    fetch_tokens.start()
+    fetch_ids.wait()
+    taken, _, _ = slot_table(ids[...], total, capacity)
     taken = taken.astype(F32).astype(BF16)
-    copy.wait()
-    out_ref[...] = jnp.dot(taken, held[...], preferred_element_type=F32).astype(BF16)
+    fetch_tokens.wait()
+    out_ref[...] = jnp.dot(taken, tokens[...], preferred_element_type=F32).astype(BF16)
 
 
 def weight_kernel(total, capacity, ids_ref, combine_ref, high_ref, low_ref):
@@ -89,9 +92,12 @@
     outgoing = pl.pallas_call(
         functools.partial(dispatch_kernel, total, capacity),
         out_shape=jax.ShapeDtypeStruct((slots, width), BF16),
-        in_specs=[pl.BlockSpec(memory_space=pltpu.VMEM), pl.BlockSpec(memory_space=pl.ANY)],
-        scratch_shapes=[pltpu.VMEM((rows, width), BF16), pltpu.SemaphoreType.DMA],
-        compiler_params=params,
+        in_specs=[pl.BlockSpec(memory_space=pltpu.HBM)] * 2,
+        scratch_shapes=[
+            pltpu.VMEM(ids_t.shape, jnp.int32),
+            pltpu.VMEM((rows, width), BF16),
+            pltpu.SemaphoreType.DMA((2,)),
+        ],
     )(ids_t, tokens)
     high, low = pl.pallas_call(
         functools.partial(weight_kernel, total, capacity),
@@ -102,9 +108,6 @@
     arrived = lax.all_to_all(
         outgoing.reshape(n_cols, block, width), "expert", split_axis=0, concat_axis=0, tiled=True
     ).reshape(slots, width)
-    both = jnp.concatenate(
-        [gate_weight.reshape(here * width, ff), up_weight.reshape(here * width, ff)], axis=1
-    )
     owner = lax.broadcasted_iota(jnp.int32, (slots, 1), 0) % block // capacity
 
     def by_expert(x):
@@ -112,10 +115,14 @@
             [jnp.where(owner == e, x, jnp.zeros((), x.dtype)) for e in range(here)], axis=1
         )
 
-    part = jnp.dot(by_expert(arrived), both, preferred_element_type=F32)
-    sums = lax.psum((part * 16.0).astype(F16), "dp")
-    gate = sums[:, :ff].astype(F32) * (1.0 / 16.0)
-    up = sums[:, ff:].astype(F32) * (1.0 / 16.0)
+    rows_in = by_expert(arrived)
+
+    def project(weight):
+        part = jnp.dot(rows_in, weight.reshape(here * width, ff), preferred_element_type=F32)
+        return (part * 16.0).astype(F16)
+
+    gate, up = lax.psum((project(gate_weight), project(up_weight)), "dp")
+    gate, up = gate.astype(F32) * (1.0 / 16.0), up.astype(F32) * (1.0 / 16.0)
     hidden = (jax.nn.silu(gate) * up).astype(BF16)
     result = pl.pallas_call(
         functools.partial(down_kernel, capacity),

time: 155 us -> 153 us (0.987)
    dot_general x1 -> x2, matrix products: 4.09 us -> 3.67 us  [project(): jnp.dot(rows_in, weight.reshape(here * width, ff), preferred_element_type...]
where the time goes in v3:
time: 153 us
  blocking collectives  95.1 us (62%)
  waiting for transfers between devices  25.1 us (16%)
  starting transfers between devices  18 us (12%)
  Pallas kernels  6.27 us (4%)
  other arithmetic  4.6 us (3%)
  matrix products  3.67 us (2%)
    psum x1, blocking collectives, per_device(): gate, up = lax.psum((project(gate_weight), project(up_weight)), 'dp')  95.1 us
    all_to_all x1, waiting for transfers between devices, per_device(): lax.all_to_all(outgoing.reshape(n_cols, block, width), 'expert', split_ax...  13 us
    all_to_all x1, waiting for transfers between devices, per_device(): lax.all_to_all(result.reshape(n_cols, block, width), 'expert', split_axis...  12.1 us
    all_to_all x1, starting transfers between devices, per_device(): lax.all_to_all(outgoing.reshape(n_cols, block, width), 'expert', split_ax...  10.4 us
    all_to_all x1, starting transfers between devices, per_device(): lax.all_to_all(result.reshape(n_cols, block, width), 'expert', split_axis...  7.53 us
    convert_element_type x1, other arithmetic, per_device(): hidden = (jax.nn.silu(gate) * up).astype(BF16)  3.73 us
    dot_general x2, matrix products, project(): jnp.dot(rows_in, weight.reshape(here * width, ff), preferred_element_type...  3.67 us
  transfers between devices with their start and end apart: 2, of which 2 were waited for; matrix products, arithmetic and copies ran while one was open for 0% of the time, Pallas kernels for 1%

profile of v3, /device:TPU:1, one launch (start us, length us, event | category | flops | bytes accessed | tf_op | source)
XLA Modules:
  0.0 152.9 jit_solution(10578754708052126150)
XLA Ops:
  0.0 0.0 copy-start
  0.0 2.5 %shard_map.65 = bf16[1280,256]{1,0:T(8,128)(2,1)} custom-call(s32[8,128]{1,0:T(8,128)} %bitcast.18, bf16[128,256]{1,0:T(8,128)(2,1)} %tokens_ref.1), custom_call_target="tpu_custom_call" | custom-call | tf_op jit(solution)/shard_map/pallas_call | solution.py:92
  2.5 10.4 %all-to-all-start = ((bf16[32,40,256]{2,1,0:T(8,128)(2,1)}), bf16[32,40,256]{2,1,0:T(8,128)(2,1)S(1)}, u32[]{:S(2)}, u32[]{:S(2)}) async-start(bf16[32,40,256]{2,1,0:T(8,128)(2,1)} %bitcast.21), calls=%async_computation | async-start | bytes 1310720 | tf_op jit(solution)/shard_map/all_to_all | solution.py:108
  13.0 13.0 %all-to-all-done = bf16[32,40,256]{2,1,0:T(8,128)(2,1)S(1)} async-done(((bf16[32,40,256]{2,1,0:T(8,128)(2,1)}), bf16[32,40,256]{2,1,0:T(8,128)(2,1)S(1)}, u32[]{:S(2)}, u32[]{:S(2)}) %all-to-all-start) | async-done | bytes 655392 | tf_op jit(solution)/shard_map/all_to_all | solution.py:108
  26.0 0.8 bitcast_select_fusion.1
  26.8 0.0 copy-done
  26.8 0.0 copy-start.4
  26.8 1.2 fusion
  28.0 0.0 copy-done.4
  28.0 2.5 %fusion.1 = f16[1280,768]{1,0:T(8,128)(2,1)} fusion(bf16[512,768]{1,0:T(8,128)(2,1)S(1)} %bitcast.26, bf16[1280,256]{1,0:T(8,128)(2,1)S(1)} %get-tuple-element.12, bf16[1280,256]{1,0:T(8,128)(2,1)S(1)} %get-tuple-element.11), kind=kOutput, calls=%fused_computation.4 | convolution fusion | flops 1011220480 | bytes 4063232 | tf_op jit(solution)/shard_map/dot_general | solution.py:121
  30.5 95.1 %all-reduce.2 = (u32[4,122880]{1,0:T(4,128)}, u32[4,122880]{1,0:T(4,128)}) all-reduce(u32[4,122880]{1,0:T(4,128)} %bitcast.23, u32[4,122880]{1,0:T(4,128)S(1)} %bitcast.22), channel_id=1, replica_groups=mesh['dp'=16,'expert'=32] {'dp'}, use_global_device_ids=true, to_apply=%region_1.2.clone | all-reduce | flops 983040 | bytes 7864320 | tf_op jit(solution)/shard_map/psum | solution.py:124
  125.6 0.0 copy-start.1
  125.6 3.7 %multiply_convert_fusion.hidden_ref = bf16[1280,768]{1,0:T(8,128)(2,1)S(1)} fusion(f16[1280,768]{1,0:T(8,128)(2,1)} %bitcast.24, f16[1280,768]{1,0:T(8,128)(2,1)} %bitcast.25), kind=kLoop, calls=%fused_computation.2 | loop fusion | flops 9830400 | bytes 5898240 | tf_op jit(solution)/shard_map/convert_element_type | solution.py:126
  129.4 0.0 copy-done.1
  129.4 0.0 copy-start.2
  129.4 0.0 copy-start.3
  129.4 2.0 %shard_map.66 = bf16[1280,256]{1,0:T(8,128)(2,1)} custom-call(bf16[1280,768]{1,0:T(8,128)(2,1)S(1)} %multiply_convert_fusion.hidden_ref, bf16[2,768,256]{2,1,0:T(8,128)(2,1)S(1)} %copy-done.1), custom_call_target="tpu_custom_call" | custom-call | tf_op jit(solution)/shard_map/pallas_call | solution.py:127
  131.4 7.5 %all-to-all-start.1 = ((bf16[32,40,256]{2,1,0:T(8,128)(2,1)}), bf16[32,40,256]{2,1,0:T(8,128)(2,1)S(1)}, u32[]{:S(2)}, u32[]{:S(2)}) async-start(bf16[32,40,256]{2,1,0:T(8,128)(2,1)} %bitcast.6), calls=%async_computation.1 | async-start | bytes 1310720 | tf_op jit(solution)/shard_map/all_to_all | solution.py:132
  139.0 0.0 copy-done.2
  139.0 0.0 copy-done.3
  139.0 0.8 shard_map.64
  139.8 12.1 %all-to-all-done.1 = bf16[32,40,256]{2,1,0:T(8,128)(2,1)S(1)} async-done(((bf16[32,40,256]{2,1,0:T(8,128)(2,1)}), bf16[32,40,256]{2,1,0:T(8,128)(2,1)S(1)}, u32[]{:S(2)}, u32[]{:S(2)}) %all-to-all-start.1) | async-done | bytes 655392 | tf_op jit(solution)/shard_map/all_to_all | solution.py:132
  151.9 1.0 shard_map.67
  (1 shorter events, 0.0 us)
Async XLA Ops:
  0.0 26.8 %copy-start = (bf16[2,256,768]{2,1,0:T(8,128)(2,1)S(1)}, bf16[2,256,768]{2,1,0:T(8,128)(2,1)}, u32[]{:S(2)}) copy-start(bf16[2,256,768]{2,1,0:T(8,128)(2,1)} %param.9) | copy-start | bytes 2359300
  2.5 23.5 %all-to-all-start = ((bf16[32,40,256]{2,1,0:T(8,128)(2,1)}), bf16[32,40,256]{2,1,0:T(8,128)(2,1)S(1)}, u32[]{:S(2)}, u32[]{:S(2)}) async-start(bf16[32,40,256]{2,1,0:T(8,128)(2,1)} %bitcast.21), calls=%async_computation | async-start | bytes 1310720 | tf_op jit(solution)/shard_map/all_to_all | solution.py:108
  26.8 1.2 copy-start.4
  125.6 3.7 %copy-start.1 = (bf16[2,768,256]{2,1,0:T(8,128)(2,1)S(1)}, bf16[2,768,256]{2,1,0:T(8,128)(2,1)}, u32[]{:S(2)}) copy-start(bf16[2,768,256]{2,1,0:T(8,128)(2,1)} %down_ref.1) | copy-start | bytes 2359300
  129.4 9.6 %copy-start.2 = (s32[128,8]{0,1:T(8,128)S(1)}, s32[128,8]{0,1:T(8,128)}, u32[]{:S(2)}) copy-start(s32[128,8]{0,1:T(8,128)} %param.7) | copy-start | bytes 12292
  129.4 9.6 %copy-start.3 = (f32[128,8]{0,1:T(8,128)S(1)}, f32[128,8]{0,1:T(8,128)}, u32[]{:S(2)}) copy-start(f32[128,8]{0,1:T(8,128)} %param.8) | copy-start | bytes 12292
  131.4 20.4 %all-to-all-start.1 = ((bf16[32,40,256]{2,1,0:T(8,128)(2,1)}), bf16[32,40,256]{2,1,0:T(8,128)(2,1)S(1)}, u32[]{:S(2)}, u32[]{:S(2)}) async-start(bf16[32,40,256]{2,1,0:T(8,128)(2,1)} %bitcast.6), calls=%async_computation.1 | async-start | bytes 1310720 | tf_op jit(solution)/shard_map/all_to_all | solution.py:132

commit v4 on v3

v4 whole, which is shorter than its diff:
```python
import functools

import jax
import jax.numpy as jnp
from jax import lax
from jax.experimental import pallas as pl
from jax.experimental.pallas import tpu as pltpu
from jax.sharding import PartitionSpec as P

F32, BF16, F16 = jnp.float32, jnp.bfloat16, jnp.float16
VMEM_LIMIT = 48 * 1024 * 1024


def slot_owner(total, capacity):
    slots = total * capacity
    first = lax.broadcasted_iota(jnp.int32, (slots, total), 1) * capacity
    slot = lax.broadcasted_iota(jnp.int32, (slots, total), 0)
    return ((slot >= first) & (slot < first + capacity)).astype(F32).astype(BF16)


def slot_offset(total, capacity, rows):
    slot = lax.broadcasted_iota(jnp.int32, (total * capacity, rows), 0).astype(F32)
    return slot - capacity * jnp.floor((slot + 0.5) * (1.0 / capacity))


def earlier_tokens(rows):
    earlier = lax.broadcasted_iota(jnp.int32, (rows, rows), 0)
    return (earlier < lax.broadcasted_iota(jnp.int32, (rows, rows), 1)).astype(F32).astype(BF16)


def places(ids_t, total, earlier):
    top, rows = ids_t.shape
    expert = lax.broadcasted_iota(jnp.int32, (total, rows), 0)
    named = [ids_t[k : k + 1, :] == expert for k in range(top)]
    member = functools.reduce(jnp.logical_or, named)
    count = jnp.dot(member.astype(F32).astype(BF16), earlier, preferred_element_type=F32)
    return jnp.where(member, count, -1.0).astype(BF16), named


def dispatch_kernel(total, capacity, ids_ref, tokens_ref, out_ref, ids, tokens, chunks, sems):
    parts, part = chunks.shape[0], chunks.shape[1]
    rows = tokens.shape[0]
    fetch_ids = pltpu.make_async_copy(ids_ref, ids, sems.at[0])
    fetch_tokens = pltpu.make_async_copy(tokens_ref, tokens, sems.at[1])
    fetch_ids.start()
    fetch_tokens.start()
    owner = slot_owner(total, capacity)
    offset = slot_offset(total, capacity, rows)
    earlier = earlier_tokens(rows)
    fetch_ids.wait()
    place, _ = places(ids[...], total, earlier)
    fetch_tokens.wait()
    held = tokens[...]
    sends = []
    for i in range(parts):
        own = slice(i * part, (i + 1) * part)
        wide = jnp.dot(owner[own], place, preferred_element_type=F32)
        taken = (wide == offset[own]).astype(F32).astype(BF16)
        chunks[i] = jnp.dot(taken, held, preferred_element_type=F32).astype(BF16)
        send = pltpu.make_async_copy(
            chunks.at[i], out_ref.at[pl.ds(i * part, part)], sems.at[2 + i]
        )
        send.start()
        sends.append(send)
    for send in sends:
        send.wait()


def weight_kernel(total, capacity, ids_ref, combine_ref, high_ref, low_ref):
    spread = slot_owner(total, capacity)
    place, named = places(ids_ref[...], total, earlier_tokens(ids_ref.shape[1]))
    wide = jnp.dot(spread, place, preferred_element_type=F32)
    taken = wide == slot_offset(total, capacity, ids_ref.shape[1])
    combine = combine_ref[...]
    weight = functools.reduce(
        jnp.add, [jnp.where(n, combine[k : k + 1, :], 0.0) for k, n in enumerate(named)]
    )
    high = weight.astype(BF16)
    low = (weight - high.astype(F32)).astype(BF16)
    for part, ref in ((high, high_ref), (low, low_ref)):
        wide = jnp.dot(spread, part, preferred_element_type=F32)
        ref[...] = jnp.where(taken, wide, 0.0).T.astype(BF16)


def down_kernel(capacity, hidden_ref, down_ref, out_ref, chunks, sems):
    here = down_ref.shape[0]
    parts, part, width = chunks.shape
    block = here * capacity
    row = lax.broadcasted_iota(jnp.int32, (part, width), 0).astype(F32)
    row = row - block * jnp.floor((row + 0.5) * (1.0 / block))
    sends = []
    for i in range(parts):
        hidden = hidden_ref[i * part : (i + 1) * part]
        out = jnp.dot(hidden, down_ref[0], preferred_element_type=F32)
        for e in range(1, here):
            other = jnp.dot(hidden, down_ref[e], preferred_element_type=F32)
            out = jnp.where(row < e * capacity, out, other)
        chunks[i] = out.astype(BF16)
        send = pltpu.make_async_copy(
            chunks.at[i], out_ref.at[pl.ds(i * part, part)], sems.at[i]
        )
        send.start()
        sends.append(send)
    for send in sends:
        send.wait()


def split_kernel(capacity, rows_ref, out_ref):
    here, width = out_ref.shape[1] // rows_ref.shape[1], rows_ref.shape[1]
    block = here * capacity
    row = lax.broadcasted_iota(jnp.int32, rows_ref.shape, 0).astype(F32)
    row = row - block * jnp.floor((row + 0.5) * (1.0 / block))
    rows = rows_ref[...]
    for e in range(here):
        own = (row >= e * capacity) & (row < (e + 1) * capacity)
        out_ref[:, e * width : (e + 1) * width] = jnp.where(own, rows, jnp.zeros((), BF16))


def mix_kernel(high_ref, low_ref, back_ref, out_ref):
    back = back_ref[...]
    out_ref[...] = (
        jnp.dot(high_ref[...], back, preferred_element_type=F32)
        + jnp.dot(low_ref[...], back, preferred_element_type=F32)
    ).astype(BF16)


def per_device(tokens, expert_ids, combine, gate_weight, up_weight, down_weight):
    n_cols = lax.axis_size("expert")
    rows, width = tokens.shape
    here, _, ff = gate_weight.shape
    capacity = rows * 5 // 32
    total = n_cols * here
    slots = total * capacity
    parts = 5
    ids_t = expert_ids.T
    params = pltpu.CompilerParams(vmem_limit_bytes=VMEM_LIMIT)
    outgoing = pl.pallas_call(
        functools.partial(dispatch_kernel, total, capacity),
        out_shape=jax.ShapeDtypeStruct((slots, width), BF16),
        in_specs=[pl.BlockSpec(memory_space=pltpu.HBM)] * 2,
        out_specs=pl.BlockSpec(memory_space=pltpu.HBM),
        scratch_shapes=[
            pltpu.VMEM(ids_t.shape, jnp.int32),
            pltpu.VMEM((rows, width), BF16),
            pltpu.VMEM((parts, slots // parts, width), BF16),
            pltpu.SemaphoreType.DMA((2 + parts,)),
        ],
    )(ids_t, tokens)
    high, low = pl.pallas_call(
        functools.partial(weight_kernel, total, capacity),
        out_shape=[jax.ShapeDtypeStruct((rows, slots), BF16)] * 2,
        compiler_params=params,
    )(ids_t, combine.T)
    block = here * capacity
    arrived = lax.all_to_all(
        outgoing.reshape(n_cols, block, width), "expert", split_axis=0, concat_axis=0, tiled=True
    ).reshape(slots, width)
    rows_in = pl.pallas_call(
        functools.partial(split_kernel, capacity),
        out_shape=jax.ShapeDtypeStruct((slots, here * width), BF16),
        compiler_params=params,
    )(arrived)

    def project(weight):
        part = jnp.dot(rows_in, weight.reshape(here * width, ff), preferred_element_type=F32)
        return (part * 16.0).astype(F16)

    gate, up = lax.psum((project(gate_weight), project(up_weight)), "dp")
    gate, up = gate.astype(F32) * (1.0 / 16.0), up.astype(F32) * (1.0 / 16.0)
    hidden = (jax.nn.silu(gate) * up).astype(BF16)
    result = pl.pallas_call(
        functools.partial(down_kernel, capacity),
        out_shape=jax.ShapeDtypeStruct((slots, width), BF16),
        in_specs=[pl.BlockSpec(memory_space=pltpu.VMEM)] * 2,
        out_specs=pl.BlockSpec(memory_space=pltpu.HBM),
        scratch_shapes=[
            pltpu.VMEM((4, slots // 4, width), BF16),
            pltpu.SemaphoreType.DMA((4,)),
        ],
        compiler_params=params,
    )(hidden, down_weight)
    returned = lax.all_to_all(
        result.reshape(n_cols, block, width), "expert", split_axis=0, concat_axis=0, tiled=True
    ).reshape(slots, width)
    return pl.pallas_call(
        mix_kernel,
        out_shape=jax.ShapeDtypeStruct((rows, width), BF16),
        compiler_params=params,
    )(high, low, returned)


def solution(mesh):
    placed = (
        P("expert", "dp"),
        P("expert", None),
        P("expert", None),
        P("expert", "dp", None),
        P("expert", "dp", None),
        P("expert", None, "dp"),
    )
    return jax.shard_map(
        per_device, mesh=mesh, in_specs=placed, out_specs=P("expert", "dp"), check_vma=False
    )
```

time: 153 us -> 153 us (level)
  blocking collectives: 95.1 us -> 118 us
  waiting for transfers between devices: 25.1 us -> 12.1 us
  starting transfers between devices: 18 us -> 7.92 us
    all_to_all x0 -> x1, blocking collectives: none -> 23.5 us  [per_device(): lax.all_to_all(outgoing.reshape(n_cols, block, width), 'expert', split_ax...]
    all_to_all x1 -> x0, waiting for transfers between devices: 13 us -> none  [per_device(): lax.all_to_all(outgoing.reshape(n_cols, block, width), 'expert', split_ax...]
    all_to_all x1 -> x0, starting transfers between devices: 10.4 us -> none  [per_device(): lax.all_to_all(outgoing.reshape(n_cols, block, width), 'expert', split_ax...]
  transfers between devices with their start and end apart: 2 -> 1, of which waited for: 2 -> 1; matrix products, arithmetic and copies ran while one was open for 0% -> 0% of each run, Pallas kernels for 1% -> 1%
where the time goes in v4:
time: 153 us; the launch traced here: 152 us
  blocking collectives  118 us (77%)
  waiting for transfers between devices  12.1 us (8%)
  starting transfers between devices  7.92 us (5%)
  Pallas kernels  6.44 us (4%)
  other arithmetic  3.73 us (2%)
  matrix products  3.65 us (2%)
    psum x1, blocking collectives, per_device(): gate, up = lax.psum((project(gate_weight), project(up_weight)), 'dp')  94.9 us
    all_to_all x1, blocking collectives, per_device(): lax.all_to_all(outgoing.reshape(n_cols, block, width), 'expert', split_ax...  23.5 us
    all_to_all x1, waiting for transfers between devices, per_device(): lax.all_to_all(result.reshape(n_cols, block, width), 'expert', split_axis...  12.1 us
    all_to_all x1, starting transfers between devices, per_device(): lax.all_to_all(result.reshape(n_cols, block, width), 'expert', split_axis...  7.92 us
    convert_element_type x1, other arithmetic, per_device(): hidden = (jax.nn.silu(gate) * up).astype(BF16)  3.73 us
    dot_general x2, matrix products, project(): jnp.dot(rows_in, weight.reshape(here * width, ff), preferred_element_type...  3.65 us
  transfers between devices with their start and end apart: 1, of which 1 were waited for; matrix products, arithmetic and copies ran while one was open for 0% of the time, Pallas kernels for 1%

profile of v4, /device:TPU:1, one launch (start us, length us, event | category | flops | bytes accessed | tf_op | source)
XLA Modules:
  0.0 152.3 jit_solution(14208359948805744836)
XLA Ops:
  0.0 0.0 copy-start
  0.0 2.4 %shard_map.65 = bf16[1280,256]{1,0:T(8,128)(2,1)} custom-call(s32[8,128]{1,0:T(8,128)} %bitcast.19, bf16[128,256]{1,0:T(8,128)(2,1)} %tokens_ref.1), custom_call_target="tpu_custom_call" | custom-call | tf_op jit(solution)/shard_map/pallas_call | solution.py:137
  2.4 23.5 %all_to_all.10 = bf16[32,40,256]{2,1,0:T(8,128)(2,1)S(1)} all-to-all(bf16[32,40,256]{2,1,0:T(8,128)(2,1)} %bitcast.22), channel_id=1, replica_groups=mesh['dp'=16,'expert'=32] {'expert'}, dimensions={0} | all-to-all | bytes 1310720 | tf_op jit(solution)/shard_map/all_to_all | solution.py:155
  25.8 0.4 shard_map.66
  26.2 0.0 copy-done
  26.2 0.0 copy-start.4
  26.3 1.2 fusion.1
  27.5 0.0 copy-done.4
  27.5 2.5 %fusion = f16[1280,768]{1,0:T(8,128)(2,1)} fusion(bf16[1280,512]{1,0:T(8,128)(2,1)S(1)} %shard_map.66, bf16[512,768]{1,0:T(8,128)(2,1)S(1)} %bitcast.27), kind=kOutput, calls=%fused_computation.3 | convolution fusion | flops 1008599040 | bytes 4063232 | tf_op jit(solution)/shard_map/dot_general | solution.py:165
  29.9 94.9 %all-reduce.2 = (u32[4,122880]{1,0:T(4,128)}, u32[4,122880]{1,0:T(4,128)}) all-reduce(u32[4,122880]{1,0:T(4,128)S(1)} %bitcast.23, u32[4,122880]{1,0:T(4,128)} %bitcast.24), channel_id=1, replica_groups=mesh['dp'=16,'expert'=32] {'dp'}, use_global_device_ids=true, to_apply=%region_1.0.clone | all-reduce | flops 983040 | bytes 7864320 | tf_op jit(solution)/shard_map/psum | solution.py:168
  124.8 0.0 copy-start.1
  124.8 3.7 %multiply_convert_fusion.hidden_ref = bf16[1280,768]{1,0:T(8,128)(2,1)S(1)} fusion(f16[1280,768]{1,0:T(8,128)(2,1)} %bitcast.25, f16[1280,768]{1,0:T(8,128)(2,1)} %bitcast.26), kind=kLoop, calls=%fused_computation.2 | loop fusion | flops 9830400 | bytes 5898240 | tf_op jit(solution)/shard_map/convert_element_type | solution.py:170
  128.5 0.0 copy-done.1
  128.5 0.0 copy-start.2
  128.5 0.0 copy-start.3
  128.6 1.9 %shard_map.67 = bf16[1280,256]{1,0:T(8,128)(2,1)} custom-call(bf16[1280,768]{1,0:T(8,128)(2,1)S(1)} %multiply_convert_fusion.hidden_ref, bf16[2,768,256]{2,1,0:T(8,128)(2,1)S(1)} %copy-done.1), custom_call_target="tpu_custom_call" | custom-call | tf_op jit(solution)/shard_map/pallas_call | solution.py:171
  130.4 7.9 %all-to-all-start.1 = ((bf16[32,40,256]{2,1,0:T(8,128)(2,1)}), bf16[32,40,256]{2,1,0:T(8,128)(2,1)S(1)}, u32[]{:S(2)}, u32[]{:S(2)}) async-start(bf16[32,40,256]{2,1,0:T(8,128)(2,1)} %bitcast.6), calls=%async_computation.1 | async-start | bytes 1310720 | tf_op jit(solution)/shard_map/all_to_all | solution.py:182
  138.4 0.0 copy-done.2
  138.4 0.0 copy-done.3
  138.4 0.8 shard_map.64
  139.2 12.1 %all-to-all-done.1 = bf16[32,40,256]{2,1,0:T(8,128)(2,1)S(1)} async-done(((bf16[32,40,256]{2,1,0:T(8,128)(2,1)}), bf16[32,40,256]{2,1,0:T(8,128)(2,1)S(1)}, u32[]{:S(2)}, u32[]{:S(2)}) %all-to-all-start.1) | async-done | bytes 655392 | tf_op jit(solution)/shard_map/all_to_all | solution.py:182
  151.3 1.0 shard_map.68
Async XLA Ops:
  0.0 26.2 %copy-start = (bf16[2,256,768]{2,1,0:T(8,128)(2,1)S(1)}, bf16[2,256,768]{2,1,0:T(8,128)(2,1)}, u32[]{:S(2)}) copy-start(bf16[2,256,768]{2,1,0:T(8,128)(2,1)} %param.10) | copy-start | bytes 2359300
  26.2 1.2 copy-start.4
  124.8 3.7 %copy-start.1 = (bf16[2,768,256]{2,1,0:T(8,128)(2,1)S(1)}, bf16[2,768,256]{2,1,0:T(8,128)(2,1)}, u32[]{:S(2)}) copy-start(bf16[2,768,256]{2,1,0:T(8,128)(2,1)} %down_ref.1) | copy-start | bytes 2359300
  128.5 9.9 %copy-start.2 = (s32[128,8]{0,1:T(8,128)S(1)}, s32[128,8]{0,1:T(8,128)}, u32[]{:S(2)}) copy-start(s32[128,8]{0,1:T(8,128)} %param.7) | copy-start | bytes 12292
  128.5 9.8 %copy-start.3 = (f32[128,8]{0,1:T(8,128)S(1)}, f32[128,8]{0,1:T(8,128)}, u32[]{:S(2)}) copy-start(f32[128,8]{0,1:T(8,128)} %param.8) | copy-start | bytes 12292
  130.4 20.8 %all-to-all-start.1 = ((bf16[32,40,256]{2,1,0:T(8,128)(2,1)}), bf16[32,40,256]{2,1,0:T(8,128)(2,1)S(1)}, u32[]{:S(2)}, u32[]{:S(2)}) async-start(bf16[32,40,256]{2,1,0:T(8,128)(2,1)} %bitcast.6), calls=%async_computation.1 | async-start | bytes 1310720 | tf_op jit(solution)/shard_map/all_to_all | solution.py:182

commit v5 on v4

--- a/solution.py
+++ b/solution.py
@@ -82,27 +82,16 @@
         ref[...] = jnp.where(taken, wide, 0.0).T.astype(BF16)
 
 
-def down_kernel(capacity, hidden_ref, down_ref, out_ref, chunks, sems):
-    here = down_ref.shape[0]
-    parts, part, width = chunks.shape
+def select_kernel(capacity, outs_ref, out_ref):
+    width = out_ref.shape[1]
+    here = outs_ref.shape[1] // width
     block = here * capacity
-    row = lax.broadcasted_iota(jnp.int32, (part, width), 0).astype(F32)
+    row = lax.broadcasted_iota(jnp.int32, out_ref.shape, 0).astype(F32)
     row = row - block * jnp.floor((row + 0.5) * (1.0 / block))
-    sends = []
-    for i in range(parts):
-        hidden = hidden_ref[i * part : (i + 1) * part]
-        out = jnp.dot(hidden, down_ref[0], preferred_element_type=F32)
-        for e in range(1, here):
-            other = jnp.dot(hidden, down_ref[e], preferred_element_type=F32)
-            out = jnp.where(row < e * capacity, out, other)
-        chunks[i] = out.astype(BF16)
-        send = pltpu.make_async_copy(
-            chunks.at[i], out_ref.at[pl.ds(i * part, part)], sems.at[i]
-        )
-        send.start()
-        sends.append(send)
-    for send in sends:
-        send.wait()
+    out = outs_ref[:, :width]
+    for e in range(1, here):
+        out = jnp.where(row < e * capacity, out, outs_ref[:, e * width : (e + 1) * width])
+    out_ref[...] = out
 
 
 def split_kernel(capacity, rows_ref, out_ref):
@@ -168,17 +157,14 @@
     gate, up = lax.psum((project(gate_weight), project(up_weight)), "dp")
     gate, up = gate.astype(F32) * (1.0 / 16.0), up.astype(F32) * (1.0 / 16.0)
     hidden = (jax.nn.silu(gate) * up).astype(BF16)
+    both = jnp.concatenate([down_weight[e] for e in range(here)], axis=1)
+    outs = jnp.dot(hidden, both, preferred_element_type=F32).astype(BF16)
     result = pl.pallas_call(
-        functools.partial(down_kernel, capacity),
+        functools.partial(select_kernel, capacity),
         out_shape=jax.ShapeDtypeStruct((slots, width), BF16),
-        in_specs=[pl.BlockSpec(memory_space=pltpu.VMEM)] * 2,
-        out_specs=pl.BlockSpec(memory_space=pltpu.HBM),
-        scratch_shapes=[
-            pltpu.VMEM((4, slots // 4, width), BF16),
-            pltpu.SemaphoreType.DMA((4,)),
-        ],
         compiler_params=params,
-    )(hidden, down_weight)
+    )(outs)
+    result, high, low = lax.optimization_barrier((result, high, low))
     returned = lax.all_to_all(
         result.reshape(n_cols, block, width), "expert", split_axis=0, concat_axis=0, tiled=True
     ).reshape(slots, width)

time: 153 us -> 151 us (0.987)
  matrix products: 3.65 us -> 7.71 us
  other arithmetic: 3.73 us -> 0 us
  blocking collectives: 118 us -> 115 us
  starting transfers between devices: 7.92 us -> 10.4 us
  Pallas kernels: 6.44 us -> 4.77 us
    dot_general x0 -> x1, matrix products: none -> 4.04 us  [per_device(): outs = jnp.dot(hidden, both, preferred_element_type=F32).astype(BF16)]
    convert_element_type x1 -> x0, other arithmetic: 3.73 us -> none  [per_device(): hidden = (jax.nn.silu(gate) * up).astype(BF16)]
    all_to_all x1, blocking collectives: 23.5 us -> 20.3 us  [per_device(): lax.all_to_all(result.reshape(n_cols, block, width), 'expert', split_axis...]
    all_to_all x1, starting transfers between devices: 7.92 us -> 10.4 us  [per_device(): lax.all_to_all(outgoing.reshape(n_cols, block, width), 'expert', split_ax...]
    pallas_call x1, Pallas kernels: 1.88 us -> 0.2 us  [per_device(): pl.pallas_call(functools.partial(select_kernel, capacity), out_shape=jax....]
  transfers between devices with their start and end apart: 1 -> 1, of which waited for: 1 -> 1; matrix products, arithmetic and copies ran while one was open for 0% -> 1% of each run, Pallas kernels for 1% -> 1%
where the time goes in v5:
time: 151 us
  blocking collectives  115 us (76%)
  waiting for transfers between devices  11.2 us (7%)
  starting transfers between devices  10.4 us (7%)
  matrix products  7.71 us (5%)
  Pallas kernels  4.77 us (3%)
    psum x1, blocking collectives, per_device(): gate, up = lax.psum((project(gate_weight), project(up_weight)), 'dp')  95.1 us
    all_to_all x1, blocking collectives, per_device(): lax.all_to_all(result.reshape(n_cols, block, width), 'expert', split_axis...  20.3 us
    all_to_all x1, waiting for transfers between devices, per_device(): lax.all_to_all(outgoing.reshape(n_cols, block, width), 'expert', split_ax...  11.2 us
    all_to_all x1, starting transfers between devices, per_device(): lax.all_to_all(outgoing.reshape(n_cols, block, width), 'expert', split_ax...  10.4 us
    dot_general x1, matrix products, per_device(): outs = jnp.dot(hidden, both, preferred_element_type=F32).astype(BF16)  4.04 us
    dot_general x2, matrix products, project(): jnp.dot(rows_in, weight.reshape(here * width, ff), preferred_element_type...  3.67 us
  transfers between devices with their start and end apart: 1, of which 1 were waited for; matrix products, arithmetic and copies ran while one was open for 1% of the time, Pallas kernels for 1%

profile of v5, /device:TPU:1, one launch (start us, length us, event | category | flops | bytes accessed | tf_op | source)
XLA Modules:
  0.0 150.6 jit_solution(3467480424908067397)
XLA Ops:
  0.0 0.0 copy-start
  0.0 0.0 copy-start.1
  0.0 0.0 copy-start.2
  0.0 0.0 copy-start.3
  0.0 2.4 %shard_map.64 = bf16[1280,256]{1,0:T(8,128)(2,1)} custom-call(s32[8,128]{1,0:T(8,128)} %bitcast.24, bf16[128,256]{1,0:T(8,128)(2,1)} %tokens_ref.1), custom_call_target="tpu_custom_call" | custom-call | tf_op jit(solution)/shard_map/pallas_call | solution.py:126
  2.5 10.4 %all-to-all-start = ((bf16[32,40,256]{2,1,0:T(8,128)(2,1)}), bf16[32,40,256]{2,1,0:T(8,128)(2,1)S(1)}, u32[]{:S(2)}, u32[]{:S(2)}) async-start(bf16[32,40,256]{2,1,0:T(8,128)(2,1)} %bitcast.27), calls=%async_computation | async-start | bytes 1310720 | tf_op jit(solution)/shard_map/all_to_all | solution.py:144
  12.9 0.0 copy-done.1
  12.9 0.0 copy-done.2
  12.9 0.8 shard_map.67
  13.7 0.0 copy-done.3
  13.7 0.9 slice_bitcast_fusion.1
  14.7 11.2 %all-to-all-done = bf16[32,40,256]{2,1,0:T(8,128)(2,1)S(1)} async-done(((bf16[32,40,256]{2,1,0:T(8,128)(2,1)}), bf16[32,40,256]{2,1,0:T(8,128)(2,1)S(1)}, u32[]{:S(2)}, u32[]{:S(2)}) %all-to-all-start) | async-done | bytes 655392 | tf_op jit(solution)/shard_map/all_to_all | solution.py:144
  25.9 0.4 shard_map.65
  26.3 0.0 copy-done
  26.3 0.0 copy-start.4
  26.3 1.2 fusion
  27.5 0.0 copy-done.4
  27.5 2.5 %fusion.1 = f16[1280,768]{1,0:T(8,128)(2,1)} fusion(bf16[1280,512]{1,0:T(8,128)(2,1)S(1)} %shard_map.65, bf16[512,768]{1,0:T(8,128)(2,1)S(1)} %bitcast.32), kind=kOutput, calls=%fused_computation.4 | convolution fusion | flops 1008599040 | bytes 4063232 | tf_op jit(solution)/shard_map/dot_general | solution.py:154
  30.0 95.1 %all-reduce.2 = (u32[4,122880]{1,0:T(4,128)}, u32[4,122880]{1,0:T(4,128)}) all-reduce(u32[4,122880]{1,0:T(4,128)} %bitcast.29, u32[4,122880]{1,0:T(4,128)S(1)} %bitcast.28), channel_id=1, replica_groups=mesh['dp'=16,'expert'=32] {'dp'}, use_global_device_ids=true, to_apply=%region_1.0.clone | all-reduce | flops 983040 | bytes 7864320 | tf_op jit(solution)/shard_map/psum | solution.py:157
  125.1 4.0 %convolution_convert_fusion.outs_ref = bf16[1280,512]{1,0:T(8,128)(2,1)S(1)} fusion(f16[1280,768]{1,0:T(8,128)(2,1)} %bitcast.30, f16[1280,768]{1,0:T(8,128)(2,1)} %bitcast.31, bf16[768,256]{1,0:T(8,128)(2,1)} %get-tuple-element.18, bf16[768,256]{1,0:T(8,128)(2,1)} %get-tuple-element.17), kind=kOutput, calls=%fused_computation.5 | convolution fusion | flops 1018691584 | bytes 6029312 | tf_op jit(solution)/shard_map/dot_general | solution.py:161
  129.1 0.2 shard_map.66
  129.4 20.3 %all_to_all.10 = bf16[32,40,256]{2,1,0:T(8,128)(2,1)S(1)} all-to-all(bf16[32,40,256]{2,1,0:T(8,128)(2,1)S(1)} %bitcast.23), channel_id=1, replica_groups=mesh['dp'=16,'expert'=32] {'expert'}, dimensions={0} | all-to-all | bytes 1310720 | tf_op jit(solution)/shard_map/all_to_all | solution.py:168
  149.6 1.0 shard_map.68
Async XLA Ops:
  0.0 26.3 %copy-start = (bf16[2,256,768]{2,1,0:T(8,128)(2,1)S(1)}, bf16[2,256,768]{2,1,0:T(8,128)(2,1)}, u32[]{:S(2)}) copy-start(bf16[2,256,768]{2,1,0:T(8,128)(2,1)} %param.9) | copy-start | bytes 2359300
  0.0 12.9 %copy-start.1 = (s32[128,8]{0,1:T(8,128)S(1)}, s32[128,8]{0,1:T(8,128)}, u32[]{:S(2)}) copy-start(s32[128,8]{0,1:T(8,128)} %param.7) | copy-start | bytes 12292
  0.0 12.9 %copy-start.2 = (f32[128,8]{0,1:T(8,128)S(1)}, f32[128,8]{0,1:T(8,128)}, u32[]{:S(2)}) copy-start(f32[128,8]{0,1:T(8,128)} %param.8) | copy-start | bytes 12292
  0.0 13.7 %copy-start.3 = (bf16[2,768,256]{2,1,0:T(8,128)(2,1)S(1)}, bf16[2,768,256]{2,1,0:T(8,128)(2,1)}, u32[]{:S(2)}) copy-start(bf16[2,768,256]{2,1,0:T(8,128)(2,1)} %param.11) | copy-start | bytes 2359300
  2.5 23.5 %all-to-all-start = ((bf16[32,40,256]{2,1,0:T(8,128)(2,1)}), bf16[32,40,256]{2,1,0:T(8,128)(2,1)S(1)}, u32[]{:S(2)}, u32[]{:S(2)}) async-start(bf16[32,40,256]{2,1,0:T(8,128)(2,1)} %bitcast.27), calls=%async_computation | async-start | bytes 1310720 | tf_op jit(solution)/shard_map/all_to_all | solution.py:144
  26.3 1.2 copy-start.4

commit v6 on v5

--- a/solution.py
+++ b/solution.py
@@ -120,7 +120,7 @@
     capacity = rows * 5 // 32
     total = n_cols * here
     slots = total * capacity
-    parts = 5
+    parts = 2
     ids_t = expert_ids.T
     params = pltpu.CompilerParams(vmem_limit_bytes=VMEM_LIMIT)
     outgoing = pl.pallas_call(

time: 151 us -> 151 us (level)
  no operation moved by 1% of the time
where the time goes in v6:
time: 151 us; the launch traced here: 150 us
  blocking collectives  115 us (76%)
  waiting for transfers between devices  11.2 us (7%)
  starting transfers between devices  10.4 us (7%)
  matrix products  7.71 us (5%)
  Pallas kernels  4.62 us (3%)
    psum x1, blocking collectives, per_device(): gate, up = lax.psum((project(gate_weight), project(up_weight)), 'dp')  95.1 us
    all_to_all x1, blocking collectives, per_device(): lax.all_to_all(result.reshape(n_cols, block, width), 'expert', split_axis...  20.2 us
    all_to_all x1, waiting for transfers between devices, per_device(): lax.all_to_all(outgoing.reshape(n_cols, block, width), 'expert', split_ax...  11.2 us
    all_to_all x1, starting transfers between devices, per_device(): lax.all_to_all(outgoing.reshape(n_cols, block, width), 'expert', split_ax...  10.4 us
    dot_general x1, matrix products, per_device(): outs = jnp.dot(hidden, both, preferred_element_type=F32).astype(BF16)  4.05 us
    dot_general x2, matrix products, project(): jnp.dot(rows_in, weight.reshape(here * width, ff), preferred_element_type...  3.67 us
  transfers between devices with their start and end apart: 1, of which 1 were waited for; matrix products, arithmetic and copies ran while one was open for 1% of the time, Pallas kernels for 1%

profile of v6, /device:TPU:1, one launch (start us, length us, event | category | flops | bytes accessed | tf_op | source)
XLA Modules:
  0.0 150.4 jit_solution(750141711276309734)
XLA Ops:
  0.0 0.0 copy-start
  0.0 0.0 copy-start.1
  0.0 0.0 copy-start.2
  0.0 0.0 copy-start.3
  0.0 2.3 %shard_map.64 = bf16[1280,256]{1,0:T(8,128)(2,1)} custom-call(s32[8,128]{1,0:T(8,128)} %bitcast.24, bf16[128,256]{1,0:T(8,128)(2,1)} %tokens_ref.1), custom_call_target="tpu_custom_call" | custom-call | tf_op jit(solution)/shard_map/pallas_call | solution.py:126
  2.3 10.4 %all-to-all-start = ((bf16[32,40,256]{2,1,0:T(8,128)(2,1)}), bf16[32,40,256]{2,1,0:T(8,128)(2,1)S(1)}, u32[]{:S(2)}, u32[]{:S(2)}) async-start(bf16[32,40,256]{2,1,0:T(8,128)(2,1)} %bitcast.27), calls=%async_computation | async-start | bytes 1310720 | tf_op jit(solution)/shard_map/all_to_all | solution.py:144
  12.7 0.0 copy-done.1
  12.8 0.0 copy-done.2
  12.8 0.8 shard_map.67
  13.6 0.0 copy-done.3
  13.6 0.9 slice_bitcast_fusion.1
  14.5 11.2 %all-to-all-done = bf16[32,40,256]{2,1,0:T(8,128)(2,1)S(1)} async-done(((bf16[32,40,256]{2,1,0:T(8,128)(2,1)}), bf16[32,40,256]{2,1,0:T(8,128)(2,1)S(1)}, u32[]{:S(2)}, u32[]{:S(2)}) %all-to-all-start) | async-done | bytes 655392 | tf_op jit(solution)/shard_map/all_to_all | solution.py:144
  25.8 0.4 shard_map.65
  26.2 0.0 copy-done
  26.2 0.0 copy-start.4
  26.2 1.2 fusion
  27.4 0.0 copy-done.4
  27.4 2.5 %fusion.1 = f16[1280,768]{1,0:T(8,128)(2,1)} fusion(bf16[1280,512]{1,0:T(8,128)(2,1)S(1)} %shard_map.65, bf16[512,768]{1,0:T(8,128)(2,1)S(1)} %bitcast.32), kind=kOutput, calls=%fused_computation.4 | convolution fusion | flops 1008599040 | bytes 4063232 | tf_op jit(solution)/shard_map/dot_general | solution.py:154
  29.9 95.1 %all-reduce.2 = (u32[4,122880]{1,0:T(4,128)}, u32[4,122880]{1,0:T(4,128)}) all-reduce(u32[4,122880]{1,0:T(4,128)} %bitcast.29, u32[4,122880]{1,0:T(4,128)S(1)} %bitcast.28), channel_id=1, replica_groups=mesh['dp'=16,'expert'=32] {'dp'}, use_global_device_ids=true, to_apply=%region_1.0.clone | all-reduce | flops 983040 | bytes 7864320 | tf_op jit(solution)/shard_map/psum | solution.py:157
  125.0 4.0 %convolution_convert_fusion.outs_ref = bf16[1280,512]{1,0:T(8,128)(2,1)S(1)} fusion(f16[1280,768]{1,0:T(8,128)(2,1)} %bitcast.30, f16[1280,768]{1,0:T(8,128)(2,1)} %bitcast.31, bf16[768,256]{1,0:T(8,128)(2,1)} %get-tuple-element.18, bf16[768,256]{1,0:T(8,128)(2,1)} %get-tuple-element.17), kind=kOutput, calls=%fused_computation.5 | convolution fusion | flops 1018691584 | bytes 6029312 | tf_op jit(solution)/shard_map/dot_general | solution.py:161
  129.0 0.2 shard_map.66
  129.2 20.2 %all_to_all.10 = bf16[32,40,256]{2,1,0:T(8,128)(2,1)S(1)} all-to-all(bf16[32,40,256]{2,1,0:T(8,128)(2,1)S(1)} %bitcast.23), channel_id=1, replica_groups=mesh['dp'=16,'expert'=32] {'expert'}, dimensions={0} | all-to-all | bytes 1310720 | tf_op jit(solution)/shard_map/all_to_all | solution.py:168
  149.5 1.0 shard_map.68
Async XLA Ops:
  0.0 26.2 %copy-start = (bf16[2,256,768]{2,1,0:T(8,128)(2,1)S(1)}, bf16[2,256,768]{2,1,0:T(8,128)(2,1)}, u32[]{:S(2)}) copy-start(bf16[2,256,768]{2,1,0:T(8,128)(2,1)} %param.9) | copy-start | bytes 2359300
  0.0 12.7 %copy-start.1 = (s32[128,8]{0,1:T(8,128)S(1)}, s32[128,8]{0,1:T(8,128)}, u32[]{:S(2)}) copy-start(s32[128,8]{0,1:T(8,128)} %param.7) | copy-start | bytes 12292
  0.0 12.8 %copy-start.2 = (f32[128,8]{0,1:T(8,128)S(1)}, f32[128,8]{0,1:T(8,128)}, u32[]{:S(2)}) copy-start(f32[128,8]{0,1:T(8,128)} %param.8) | copy-start | bytes 12292
  0.0 13.5 %copy-start.3 = (bf16[2,768,256]{2,1,0:T(8,128)(2,1)S(1)}, bf16[2,768,256]{2,1,0:T(8,128)(2,1)}, u32[]{:S(2)}) copy-start(bf16[2,768,256]{2,1,0:T(8,128)(2,1)} %param.11) | copy-start | bytes 2359300
  2.3 23.5 %all-to-all-start = ((bf16[32,40,256]{2,1,0:T(8,128)(2,1)}), bf16[32,40,256]{2,1,0:T(8,128)(2,1)S(1)}, u32[]{:S(2)}, u32[]{:S(2)}) async-start(bf16[32,40,256]{2,1,0:T(8,128)(2,1)} %bitcast.27), calls=%async_computation | async-start | bytes 1310720 | tf_op jit(solution)/shard_map/all_to_all | solution.py:144
  26.2 1.2 copy-start.4

commit v7 on v6

--- a/solution.py
+++ b/solution.py
@@ -82,16 +82,27 @@
         ref[...] = jnp.where(taken, wide, 0.0).T.astype(BF16)
 
 
-def select_kernel(capacity, outs_ref, out_ref):
+def beside_kernel(left_ref, right_ref, out_ref):
+    width = left_ref.shape[1]
+    out_ref[:, :width] = left_ref[...]
+    out_ref[:, width:] = right_ref[...]
+
+
+def select_kernel(capacity, *refs):
+    out_ref = refs[-1]
     width = out_ref.shape[1]
-    here = outs_ref.shape[1] // width
-    block = here * capacity
-    row = lax.broadcasted_iota(jnp.int32, out_ref.shape, 0).astype(F32)
-    row = row - block * jnp.floor((row + 0.5) * (1.0 / block))
-    out = outs_ref[:, :width]
-    for e in range(1, here):
-        out = jnp.where(row < e * capacity, out, outs_ref[:, e * width : (e + 1) * width])
-    out_ref[...] = out
+    start = 0
+    for outs_ref in refs[:-1]:
+        rows, wide = outs_ref.shape
+        here = wide // width
+        block = here * capacity
+        row = lax.broadcasted_iota(jnp.int32, (rows, width), 0).astype(F32)
+        row = row - block * jnp.floor((row + 0.5) * (1.0 / block))
+        out = outs_ref[:, :width]
+        for e in range(1, here):
+            out = jnp.where(row < e * capacity, out, outs_ref[:, e * width : (e + 1) * width])
+        out_ref[start : start + rows] = out
+        start += rows
 
 
 def split_kernel(capacity, rows_ref, out_ref):
@@ -150,20 +161,30 @@
         compiler_params=params,
     )(arrived)
 
-    def project(weight):
-        part = jnp.dot(rows_in, weight.reshape(here * width, ff), preferred_element_type=F32)
+    halves = pl.pallas_call(
+        beside_kernel,
+        out_shape=jax.ShapeDtypeStruct((here * width, 2 * ff), BF16),
+        compiler_params=params,
+    )(gate_weight.reshape(here * width, ff), up_weight.reshape(here * width, ff))
+    both = jnp.concatenate([down_weight[e] for e in range(here)], axis=1)
+
+    def project(rows_part):
+        part = jnp.dot(rows_part, halves, preferred_element_type=F32)
         return (part * 16.0).astype(F16)
 
-    gate, up = lax.psum((project(gate_weight), project(up_weight)), "dp")
-    gate, up = gate.astype(F32) * (1.0 / 16.0), up.astype(F32) * (1.0 / 16.0)
-    hidden = (jax.nn.silu(gate) * up).astype(BF16)
-    both = jnp.concatenate([down_weight[e] for e in range(here)], axis=1)
-    outs = jnp.dot(hidden, both, preferred_element_type=F32).astype(BF16)
+    def expert_outs(sums):
+        gate = sums[:, :ff].astype(F32) * (1.0 / 16.0)
+        up = sums[:, ff:].astype(F32) * (1.0 / 16.0)
+        hidden = (jax.nn.silu(gate) * up).astype(BF16)
+        return jnp.dot(hidden, both, preferred_element_type=F32).astype(BF16)
+
+    cut = n_cols * 11 // 16 * block
+    sums = lax.psum((project(rows_in[:cut]), project(rows_in[cut:])), "dp")
     result = pl.pallas_call(
         functools.partial(select_kernel, capacity),
         out_shape=jax.ShapeDtypeStruct((slots, width), BF16),
         compiler_params=params,
-    )(outs)
+    )(*[expert_outs(part) for part in sums])
     result, high, low = lax.optimization_barrier((result, high, low))
     returned = lax.all_to_all(
         result.reshape(n_cols, block, width), "expert", split_axis=0, concat_axis=0, tiled=True

time: 151 us -> 151 us (level)
  local copies, waits for them, and re-layouts: 0.97 us -> 3.95 us
  waiting for transfers between devices: 11.2 us -> 8.25 us
    all_to_all x1, waiting for transfers between devices: 11.2 us -> 8.25 us  [per_device(): lax.all_to_all(outgoing.reshape(n_cols, block, width), 'expert', split_ax...]
    unnamed x10 -> x20, local copies, waits for them, and re-layouts: 0.02 us -> 2.99 us
    dot_general x3 -> x4, matrix products: 7.71 us -> 7.11 us  [the longest x2 3.89 us: project(): part = jnp.dot(rows_part, halves, preferred_element_type=F32)]
where the time goes in v7:
time: 151 us; the launch traced here: 150 us
  blocking collectives  116 us (77%)
  starting transfers between devices  10.4 us (7%)
  waiting for transfers between devices  8.25 us (5%)
  matrix products  7.11 us (5%)
  Pallas kernels  4.66 us (3%)
  local copies, waits for them, and re-layouts  3.95 us (3%)
    psum x1, blocking collectives, per_device(): sums = lax.psum((project(rows_in[:cut]), project(rows_in[cut:])), 'dp')  95.1 us
    all_to_all x1, blocking collectives, per_device(): lax.all_to_all(result.reshape(n_cols, block, width), 'expert', split_axis...  20.6 us
    all_to_all x1, starting transfers between devices, per_device(): lax.all_to_all(outgoing.reshape(n_cols, block, width), 'expert', split_ax...  10.4 us
    all_to_all x1, waiting for transfers between devices, per_device(): lax.all_to_all(outgoing.reshape(n_cols, block, width), 'expert', split_ax...  8.25 us
    dot_general x2, matrix products, project(): part = jnp.dot(rows_part, halves, preferred_element_type=F32)  3.89 us
    dot_general x2, matrix products, expert_outs(): return jnp.dot(hidden, both, preferred_element_type=F32).astype(BF16)  3.22 us
  transfers between devices with their start and end apart: 1, of which 1 were waited for; matrix products, arithmetic and copies ran while one was open for 1% of the time, Pallas kernels for 1%

profile of v7, /device:TPU:1, one launch (start us, length us, event | category | flops | bytes accessed | tf_op | source)
XLA Modules:
  0.0 150.2 jit_solution(9081910710757253297)
XLA Ops:
  0.0 0.0 copy-start.4
  0.0 0.0 copy-start.5
  0.0 0.0 copy-start
  0.0 2.2 %shard_map.64 = bf16[1280,256]{1,0:T(8,128)(2,1)} custom-call(s32[8,128]{1,0:T(8,128)} %bitcast.23, bf16[128,256]{1,0:T(8,128)(2,1)} %tokens_ref.1), custom_call_target="tpu_custom_call" | custom-call | tf_op jit(solution)/shard_map/pallas_call | solution.py:137
  2.3 10.4 %all-to-all-start = ((bf16[32,40,256]{2,1,0:T(8,128)(2,1)}), bf16[32,40,256]{2,1,0:T(8,128)(2,1)S(1)}, u32[]{:S(2)}, u32[]{:S(2)}) async-start(bf16[32,40,256]{2,1,0:T(8,128)(2,1)} %bitcast.27), calls=%async_computation | async-start | bytes 1310720 | tf_op jit(solution)/shard_map/all_to_all | solution.py:155
  12.7 0.0 copy-done.4
  12.7 0.0 copy-done.5
  12.7 0.8 shard_map.68
  13.5 0.0 copy-start.2
  13.5 0.7 copy-done.2
  14.2 0.0 copy-done
  14.2 0.0 copy-start.1
  14.2 1.1 copy-done.1
  15.4 0.0 copy-start.6
  15.4 0.1 shard_map.66
  15.5 1.0 copy-done.6
  16.5 1.0 slice_bitcast_fusion.1
  17.5 8.3 %all-to-all-done = bf16[32,40,256]{2,1,0:T(8,128)(2,1)S(1)} async-done(((bf16[32,40,256]{2,1,0:T(8,128)(2,1)}), bf16[32,40,256]{2,1,0:T(8,128)(2,1)S(1)}, u32[]{:S(2)}, u32[]{:S(2)}) %all-to-all-start) | async-done | bytes 655392 | tf_op jit(solution)/shard_map/all_to_all | solution.py:155
  25.7 0.4 shard_map.65
  26.1 3.1 %multiply_convert_fusion = f16[880,1536]{1,0:T(8,128)(2,1)} fusion(bf16[512,1536]{1,0:T(8,128)(2,1)S(1)} %shard_map.66, bf16[1280,512]{1,0:T(8,128)(2,1)S(1)} %shard_map.65), kind=kOutput, calls=%fused_computation | convolution fusion | flops 1386823680 | bytes 5177344 | tf_op jit(solution)/shard_map/dot_general | solution.py:172
  29.2 0.8 fusion
  30.0 0.0 copy-start.7
  30.0 0.0 copy-start.8
  30.0 95.1 %all-reduce.2 = (u32[4,168960]{1,0:T(4,128)}, u32[4,76800]{1,0:T(4,128)}) all-reduce(u32[4,168960]{1,0:T(4,128)} %bitcast.26, u32[4,76800]{1,0:T(4,128)S(1)} %bitcast.28), channel_id=1, replica_groups=mesh['dp'=16,'expert'=32] {'dp'}, use_global_device_ids=true, to_apply=%region_0.0.clone | all-reduce | flops 983040 | bytes 7864320 | tf_op jit(solution)/shard_map/psum | solution.py:182
  125.1 0.0 copy-done.7
  125.1 0.0 copy-done.8
  125.1 0.0 copy-start.9
  125.1 2.0 %convolution_convert_fusion.1.refs_1_ = bf16[400,512]{1,0:T(8,128)(2,1)S(1)} fusion(f16[400,1536]{1,0:T(8,128)(2,1)} %bitcast.30, bf16[768,256]{1,0:T(8,128)(2,1)S(1)} %copy-done.8, bf16[768,256]{1,0:T(8,128)(2,1)S(1)} %copy-done.7), kind=kOutput, calls=%fused_computation.5 | convolution fusion | flops 319422464 | bytes 2424832 | tf_op jit(solution)/shard_map/dot_general | solution.py:179
  127.1 0.1 copy-done.9
  127.2 1.2 convolution_convert_fusion.refs_0_
  128.4 0.0 copy-start.3
  128.4 0.2 shard_map.67
  128.6 20.6 %all_to_all.10 = bf16[32,40,256]{2,1,0:T(8,128)(2,1)S(1)} all-to-all(bf16[32,40,256]{2,1,0:T(8,128)(2,1)S(1)} %bitcast.20), channel_id=1, replica_groups=mesh['dp'=16,'expert'=32] {'expert'}, dimensions={0} | all-to-all | bytes 1310720 | tf_op jit(solution)/shard_map/all_to_all | solution.py:189
  149.2 0.0 copy-done.3
  149.2 1.0 shard_map.69
Async XLA Ops:
  0.0 12.7 %copy-start.4 = (s32[128,8]{0,1:T(8,128)S(1)}, s32[128,8]{0,1:T(8,128)}, u32[]{:S(2)}) copy-start(s32[128,8]{0,1:T(8,128)} %param.7) | copy-start | bytes 12292
  0.0 12.7 %copy-start.5 = (f32[128,8]{0,1:T(8,128)S(1)}, f32[128,8]{0,1:T(8,128)}, u32[]{:S(2)}) copy-start(f32[128,8]{0,1:T(8,128)} %param.8) | copy-start | bytes 12292
  0.0 14.2 %copy-start = (bf16[2,256,768]{2,1,0:T(8,128)(2,1)S(1)}, bf16[2,256,768]{2,1,0:T(8,128)(2,1)}, u32[]{:S(2)}) copy-start(bf16[2,256,768]{2,1,0:T(8,128)(2,1)} %param.9) | copy-start | bytes 2359300
  2.3 23.5 %all-to-all-start = ((bf16[32,40,256]{2,1,0:T(8,128)(2,1)}), bf16[32,40,256]{2,1,0:T(8,128)(2,1)S(1)}, u32[]{:S(2)}, u32[]{:S(2)}) async-start(bf16[32,40,256]{2,1,0:T(8,128)(2,1)} %bitcast.27), calls=%async_computation | async-start | bytes 1310720 | tf_op jit(solution)/shard_map/all_to_all | solution.py:155
  13.5 0.7 copy-start.2
  14.2 1.1 copy-start.1
  15.4 1.1 copy-start.6
  30.0 95.1 %copy-start.7 = (bf16[768,256]{1,0:T(8,128)(2,1)S(1)}, bf16[768,256]{1,0:T(8,128)(2,1)}, u32[]{:S(2)}) copy-start(bf16[768,256]{1,0:T(8,128)(2,1)} %get-tuple-element.17) | copy-start | bytes 1179652
  30.0 95.1 %copy-start.8 = (bf16[768,256]{1,0:T(8,128)(2,1)S(1)}, bf16[768,256]{1,0:T(8,128)(2,1)}, u32[]{:S(2)}) copy-start(bf16[768,256]{1,0:T(8,128)(2,1)} %get-tuple-element.18) | copy-start | bytes 1179652
  125.1 2.1 %copy-start.9 = (u32[4,168960]{1,0:T(4,128)S(1)}, u32[4,168960]{1,0:T(4,128)}, u32[]{:S(2)}) copy-start(u32[4,168960]{1,0:T(4,128)} %get-tuple-element.15) | copy-start | bytes 8110084
  128.4 20.7 %copy-start.3 = (bf16[128,1280]{1,0:T(8,128)(2,1)S(1)}, bf16[128,1280]{1,0:T(8,128)(2,1)}, u32[]{:S(2)}) copy-start(bf16[128,1280]{1,0:T(8,128)(2,1)} %copy-done.2) | copy-start | bytes 983044

commit v8 on v7

--- a/solution.py
+++ b/solution.py
@@ -178,7 +178,7 @@
         hidden = (jax.nn.silu(gate) * up).astype(BF16)
         return jnp.dot(hidden, both, preferred_element_type=F32).astype(BF16)
 
-    cut = n_cols * 11 // 16 * block
+    cut = n_cols * 12 // 16 * block
     sums = lax.psum((project(rows_in[:cut]), project(rows_in[cut:])), "dp")
     result = pl.pallas_call(
         functools.partial(select_kernel, capacity),

time: 151 us -> 150 us (level)
    unnamed x20 -> x18, local copies, waits for them, and re-layouts: 2.99 us -> 3.17 us
where the time goes in v8:
time: 150 us
  blocking collectives  116 us (77%)
  starting transfers between devices  10.4 us (7%)
  waiting for transfers between devices  8.18 us (5%)
  matrix products  5.83 us (4%)
  local copies, waits for them, and re-layouts  5.23 us (3%)
  Pallas kernels  4.67 us (3%)
    psum x1, blocking collectives, per_device(): sums = lax.psum((project(rows_in[:cut]), project(rows_in[cut:])), 'dp')  95.1 us
    all_to_all x1, blocking collectives, per_device(): lax.all_to_all(result.reshape(n_cols, block, width), 'expert', split_axis...  20.5 us
    all_to_all x1, starting transfers between devices, per_device(): lax.all_to_all(outgoing.reshape(n_cols, block, width), 'expert', split_ax...  10.4 us
    all_to_all x1, waiting for transfers between devices, per_device(): lax.all_to_all(outgoing.reshape(n_cols, block, width), 'expert', split_ax...  8.18 us
    dot_general x2, matrix products, project(): part = jnp.dot(rows_part, halves, preferred_element_type=F32)  4 us
    unnamed x18, local copies, waits for them, and re-layouts  3.17 us
  transfers between devices with their start and end apart: 1, of which 1 were waited for; matrix products, arithmetic and copies ran while one was open for 1% of the time, Pallas kernels for 1%

profile of v8, /device:TPU:1, one launch (start us, length us, event | category | flops | bytes accessed | tf_op | source)
XLA Modules:
  0.0 150.1 jit_solution(5267154664096661545)
XLA Ops:
  0.0 0.0 copy-start.4
  0.0 0.0 copy-start.5
  0.0 0.0 copy-start
  0.0 2.2 %shard_map.64 = bf16[1280,256]{1,0:T(8,128)(2,1)} custom-call(s32[8,128]{1,0:T(8,128)} %bitcast.23, bf16[128,256]{1,0:T(8,128)(2,1)} %tokens_ref.1), custom_call_target="tpu_custom_call" | custom-call | tf_op jit(solution)/shard_map/pallas_call | solution.py:137
  2.3 10.4 %all-to-all-start = ((bf16[32,40,256]{2,1,0:T(8,128)(2,1)}), bf16[32,40,256]{2,1,0:T(8,128)(2,1)S(1)}, u32[]{:S(2)}, u32[]{:S(2)}) async-start(bf16[32,40,256]{2,1,0:T(8,128)(2,1)} %bitcast.27), calls=%async_computation | async-start | bytes 1310720 | tf_op jit(solution)/shard_map/all_to_all | solution.py:155
  12.7 0.0 copy-done.4
  12.7 0.0 copy-done.5
  12.7 0.8 shard_map.68
  13.5 0.0 copy-start.2
  13.5 0.7 copy-done.2
  14.2 0.0 copy-done
  14.2 0.0 copy-start.1
  14.2 1.1 copy-done.1
  15.4 0.1 shard_map.66
  15.5 2.1 %slice_bitcast_fusion.1 = (bf16[768,256]{1,0:T(8,128)(2,1)}, bf16[768,256]{1,0:T(8,128)(2,1)}) fusion(bf16[2,768,256]{2,1,0:T(8,128)(2,1)} %param.11), kind=kLoop, calls=%fused_computation.15 | loop fusion | bytes 1572864 | tf_op jit(solution)/shard_map/squeeze | solution.py:169
  17.5 8.2 %all-to-all-done = bf16[32,40,256]{2,1,0:T(8,128)(2,1)S(1)} async-done(((bf16[32,40,256]{2,1,0:T(8,128)(2,1)}), bf16[32,40,256]{2,1,0:T(8,128)(2,1)S(1)}, u32[]{:S(2)}, u32[]{:S(2)}) %all-to-all-start) | async-done | bytes 655392 | tf_op jit(solution)/shard_map/all_to_all | solution.py:155
  25.7 0.4 shard_map.65
  26.1 3.3 %multiply_convert_fusion = f16[960,1536]{1,0:T(8,128)(2,1)} fusion(bf16[512,1536]{1,0:T(8,128)(2,1)S(1)} %shard_map.66, bf16[1280,512]{1,0:T(8,128)(2,1)S(1)} %shard_map.65), kind=kOutput, calls=%fused_computation | convolution fusion | flops 1512898560 | bytes 5505024 | tf_op jit(solution)/shard_map/dot_general | solution.py:172
  29.4 0.7 fusion
  30.1 0.0 copy-start.6
  30.1 0.0 copy-start.7
  30.1 95.1 %all-reduce.2 = (u32[4,184320]{1,0:T(4,128)}, u32[4,61440]{1,0:T(4,128)S(1)}) all-reduce(u32[4,184320]{1,0:T(4,128)} %bitcast.26, u32[4,61440]{1,0:T(4,128)S(1)} %bitcast.28), channel_id=1, replica_groups=mesh['dp'=16,'expert'=32] {'dp'}, use_global_device_ids=true, to_apply=%region_0.0.clone | all-reduce | flops 983040 | bytes 7864320 | tf_op jit(solution)/shard_map/psum | solution.py:182
  125.2 0.0 copy-done.6
  125.2 0.0 copy-done.7
  125.2 0.0 copy-start.8
  125.2 0.5 convolution_convert_fusion.refs_1_
  125.8 1.3 copy-done.8
  127.1 1.3 fusion.2.refs_0_
  128.4 0.0 copy-start.3
  128.4 0.2 shard_map.67
  128.6 20.5 %all_to_all.10 = bf16[32,40,256]{2,1,0:T(8,128)(2,1)S(1)} all-to-all(bf16[32,40,256]{2,1,0:T(8,128)(2,1)S(1)} %bitcast.20), channel_id=1, replica_groups=mesh['dp'=16,'expert'=32] {'expert'}, dimensions={0} | all-to-all | bytes 1310720 | tf_op jit(solution)/shard_map/all_to_all | solution.py:189
  149.1 0.0 copy-done.3
  149.1 1.0 shard_map.69
Async XLA Ops:
  0.0 12.7 %copy-start.4 = (s32[128,8]{0,1:T(8,128)S(1)}, s32[128,8]{0,1:T(8,128)}, u32[]{:S(2)}) copy-start(s32[128,8]{0,1:T(8,128)} %param.7) | copy-start | bytes 12292
  0.0 12.7 %copy-start.5 = (f32[128,8]{0,1:T(8,128)S(1)}, f32[128,8]{0,1:T(8,128)}, u32[]{:S(2)}) copy-start(f32[128,8]{0,1:T(8,128)} %param.8) | copy-start | bytes 12292
  0.0 14.2 %copy-start = (bf16[2,256,768]{2,1,0:T(8,128)(2,1)S(1)}, bf16[2,256,768]{2,1,0:T(8,128)(2,1)}, u32[]{:S(2)}) copy-start(bf16[2,256,768]{2,1,0:T(8,128)(2,1)} %param.9) | copy-start | bytes 2359300
  2.3 23.5 %all-to-all-start = ((bf16[32,40,256]{2,1,0:T(8,128)(2,1)}), bf16[32,40,256]{2,1,0:T(8,128)(2,1)S(1)}, u32[]{:S(2)}, u32[]{:S(2)}) async-start(bf16[32,40,256]{2,1,0:T(8,128)(2,1)} %bitcast.27), calls=%async_computation | async-start | bytes 1310720 | tf_op jit(solution)/shard_map/all_to_all | solution.py:155
  13.5 0.7 copy-start.2
  14.2 1.1 copy-start.1
  30.1 95.1 %copy-start.6 = (bf16[768,256]{1,0:T(8,128)(2,1)S(1)}, bf16[768,256]{1,0:T(8,128)(2,1)}, u32[]{:S(2)}) copy-start(bf16[768,256]{1,0:T(8,128)(2,1)} %get-tuple-element.17) | copy-start | bytes 1179652
  30.1 95.1 %copy-start.7 = (bf16[768,256]{1,0:T(8,128)(2,1)S(1)}, bf16[768,256]{1,0:T(8,128)(2,1)}, u32[]{:S(2)}) copy-start(bf16[768,256]{1,0:T(8,128)(2,1)} %get-tuple-element.18) | copy-start | bytes 1179652
  125.2 1.8 %copy-start.8 = (u32[4,184320]{1,0:T(4,128)S(1)}, u32[4,184320]{1,0:T(4,128)}, u32[]{:S(2)}) copy-start(u32[4,184320]{1,0:T(4,128)} %get-tuple-element.15) | copy-start | bytes 8847364
  128.4 20.7 %copy-start.3 = (bf16[128,1280]{1,0:T(8,128)(2,1)S(1)}, bf16[128,1280]{1,0:T(8,128)(2,1)}, u32[]{:S(2)}) copy-start(bf16[128,1280]{1,0:T(8,128)(2,1)} %copy-done.2) | copy-start | bytes 983044

commit v9 on v8

--- a/solution.py
+++ b/solution.py
@@ -82,10 +82,11 @@
         ref[...] = jnp.where(taken, wide, 0.0).T.astype(BF16)
 
 
-def beside_kernel(left_ref, right_ref, out_ref):
-    width = left_ref.shape[1]
-    out_ref[:, :width] = left_ref[...]
-    out_ref[:, width:] = right_ref[...]
+def beside_kernel(*refs):
+    out_ref = refs[-1]
+    width = refs[0].shape[1]
+    for i, ref in enumerate(refs[:-1]):
+        out_ref[:, i * width : (i + 1) * width] = ref[...]
 
 
 def select_kernel(capacity, *refs):
@@ -166,7 +167,11 @@
         out_shape=jax.ShapeDtypeStruct((here * width, 2 * ff), BF16),
         compiler_params=params,
     )(gate_weight.reshape(here * width, ff), up_weight.reshape(here * width, ff))
-    both = jnp.concatenate([down_weight[e] for e in range(here)], axis=1)
+    both = pl.pallas_call(
+        beside_kernel,
+        out_shape=jax.ShapeDtypeStruct((ff, here * width), BF16),
+        compiler_params=params,
+    )(*[down_weight[e] for e in range(here)])
 
     def project(rows_part):
         part = jnp.dot(rows_part, halves, preferred_element_type=F32)

time: 150 us -> 151 us (level)
    unnamed x18 -> x16, local copies, waits for them, and re-layouts: 3.17 us -> 5.64 us
    squeeze x1, local copies, waits for them, and re-layouts: 2.06 us -> 0.05 us  [per_device(): down_weight[e]]
  transfers between devices with their start and end apart: 1 -> 1, of which waited for: 1 -> 1; matrix products, arithmetic and copies ran while one was open for 1% -> 0% of each run, Pallas kernels for 1% -> 1%
where the time goes in v9:
time: 151 us
  blocking collectives  115 us (76%)
  starting transfers between devices  10.4 us (7%)
  waiting for transfers between devices  7.62 us (5%)
  matrix products  6.77 us (4%)
  local copies, waits for them, and re-layouts  5.7 us (4%)
  Pallas kernels  4.72 us (3%)
    psum x1, blocking collectives, per_device(): sums = lax.psum((project(rows_in[:cut]), project(rows_in[cut:])), 'dp')  95 us
    all_to_all x1, blocking collectives, per_device(): lax.all_to_all(result.reshape(n_cols, block, width), 'expert', split_axis...  20.5 us
    all_to_all x1, starting transfers between devices, per_device(): lax.all_to_all(outgoing.reshape(n_cols, block, width), 'expert', split_ax...  10.4 us
    all_to_all x1, waiting for transfers between devices, per_device(): lax.all_to_all(outgoing.reshape(n_cols, block, width), 'expert', split_ax...  7.62 us
    unnamed x16, local copies, waits for them, and re-layouts  5.64 us
    dot_general x2, matrix products, project(): part = jnp.dot(rows_part, halves, preferred_element_type=F32)  4.94 us
  transfers between devices with their start and end apart: 1, of which 1 were waited for; matrix products, arithmetic and copies ran while one was open for 0% of the time, Pallas kernels for 1%

profile of v9, /device:TPU:1, one launch (start us, length us, event | category | flops | bytes accessed | tf_op | source)
XLA Modules:
  0.0 150.8 jit_solution(6071108140890828737)
XLA Ops:
  0.0 0.0 copy-start.6
  0.0 2.2 %shard_map.64 = bf16[1280,256]{1,0:T(8,128)(2,1)} custom-call(s32[8,128]{1,0:T(8,128)} %bitcast.25, bf16[128,256]{1,0:T(8,128)(2,1)} %tokens_ref.1), custom_call_target="tpu_custom_call" | custom-call | tf_op jit(solution)/shard_map/pallas_call | solution.py:138
  2.2 10.4 %all-to-all-start = ((bf16[32,40,256]{2,1,0:T(8,128)(2,1)}), bf16[32,40,256]{2,1,0:T(8,128)(2,1)S(1)}, u32[]{:S(2)}, u32[]{:S(2)}) async-start(bf16[32,40,256]{2,1,0:T(8,128)(2,1)} %bitcast.29), calls=%async_computation | async-start | bytes 1310720 | tf_op jit(solution)/shard_map/all_to_all | solution.py:156
  12.7 0.0 copy-start.4
  12.7 0.7 copy-done.4
  13.4 0.0 copy-start.5
  13.4 0.7 copy-done.5
  14.1 0.8 shard_map.69
  14.9 0.0 copy-start.2
  14.9 0.7 copy-done.2
  15.6 0.0 copy-start
  15.6 1.1 copy-done
  16.7 0.0 copy-start.1
  16.7 1.1 copy-done.1
  17.8 0.1 shard_map.66
  18.0 0.0 copy-done.6
  18.0 0.1 slice_bitcast_fusion
  18.0 0.1 shard_map.67
  18.1 7.6 %all-to-all-done = bf16[32,40,256]{2,1,0:T(8,128)(2,1)S(1)} async-done(((bf16[32,40,256]{2,1,0:T(8,128)(2,1)}), bf16[32,40,256]{2,1,0:T(8,128)(2,1)S(1)}, u32[]{:S(2)}, u32[]{:S(2)}) %all-to-all-start) | async-done | bytes 655392 | tf_op jit(solution)/shard_map/all_to_all | solution.py:156
  25.7 0.4 shard_map.65
  26.1 3.3 %multiply_convert_fusion = f16[960,1536]{1,0:T(8,128)(2,1)} fusion(bf16[512,1536]{1,0:T(8,128)(2,1)S(1)} %shard_map.66, bf16[1280,512]{1,0:T(8,128)(2,1)S(1)} %shard_map.65), kind=kOutput, calls=%fused_computation | convolution fusion | flops 1512898560 | bytes 5505024 | tf_op jit(solution)/shard_map/dot_general | solution.py:177
  29.4 1.6 %fusion = f16[320,1536]{1,0:T(8,128)(2,1)} fusion(bf16[512,1536]{1,0:T(8,128)(2,1)S(1)} %shard_map.66, bf16[1280,512]{1,0:T(8,128)(2,1)S(1)} %shard_map.65), kind=kOutput, calls=%fused_computation.3 | convolution fusion | flops 504299520 | bytes 2883584 | tf_op jit(solution)/shard_map/dot_general | solution.py:177
  31.0 95.0 %all-reduce.2 = (u32[4,184320]{1,0:T(4,128)}, u32[4,61440]{1,0:T(4,128)S(1)}) all-reduce(u32[4,184320]{1,0:T(4,128)} %bitcast.28, u32[4,61440]{1,0:T(4,128)} %bitcast.30), channel_id=1, replica_groups=mesh['dp'=16,'expert'=32] {'dp'}, use_global_device_ids=true, to_apply=%region_0.0.clone | all-reduce | flops 983040 | bytes 7864320 | tf_op jit(solution)/shard_map/psum | solution.py:187
  126.0 0.0 copy-start.7
  126.0 0.5 convolution_convert_fusion.refs_1_
  126.5 1.3 copy-done.7
  127.8 1.3 fusion.2.refs_0_
  129.1 0.0 copy-start.3
  129.1 0.2 shard_map.68
  129.3 20.5 %all_to_all.10 = bf16[32,40,256]{2,1,0:T(8,128)(2,1)S(1)} all-to-all(bf16[32,40,256]{2,1,0:T(8,128)(2,1)S(1)} %bitcast.22), channel_id=1, replica_groups=mesh['dp'=16,'expert'=32] {'expert'}, dimensions={0} | all-to-all | bytes 1310720 | tf_op jit(solution)/shard_map/all_to_all | solution.py:194
  149.9 0.0 copy-done.3
  149.9 1.0 shard_map.70
Async XLA Ops:
  0.0 18.0 %copy-start.6 = (bf16[2,768,256]{2,1,0:T(8,128)(2,1)S(1)}, bf16[2,768,256]{2,1,0:T(8,128)(2,1)}, u32[]{:S(2)}) copy-start(bf16[2,768,256]{2,1,0:T(8,128)(2,1)} %param.11) | copy-start | bytes 2359300
  2.2 23.5 %all-to-all-start = ((bf16[32,40,256]{2,1,0:T(8,128)(2,1)}), bf16[32,40,256]{2,1,0:T(8,128)(2,1)S(1)}, u32[]{:S(2)}, u32[]{:S(2)}) async-start(bf16[32,40,256]{2,1,0:T(8,128)(2,1)} %bitcast.29), calls=%async_computation | async-start | bytes 1310720 | tf_op jit(solution)/shard_map/all_to_all | solution.py:156
  12.7 0.7 copy-start.4
  13.4 0.7 copy-start.5
  14.9 0.7 copy-start.2
  15.6 1.1 copy-start
  16.7 1.1 copy-start.1
  126.0 1.8 %copy-start.7 = (u32[4,184320]{1,0:T(4,128)S(1)}, u32[4,184320]{1,0:T(4,128)}, u32[]{:S(2)}) copy-start(u32[4,184320]{1,0:T(4,128)} %get-tuple-element.15) | copy-start | bytes 8847364
  129.1 20.7 %copy-start.3 = (bf16[128,1280]{1,0:T(8,128)(2,1)S(1)}, bf16[128,1280]{1,0:T(8,128)(2,1)}, u32[]{:S(2)}) copy-start(bf16[128,1280]{1,0:T(8,128)(2,1)} %copy-done.2) | copy-start | bytes 983044
